TPU v7x, 32 devices: a whole 2x2x4 slice. The times are simulated.
32 devices in a mesh: gx: 4 (over y, x), gy: 8 (over z, core).
Axes of the slice: x: 2, y: 2, z: 4, core: 2. Of those that a mesh axis runs over, the one named last changes fastest.
Arguments:
- right_side: float32 [16, 1024, 1024], P(None, 'gy', 'gx'), may hold values from -8 to 8
- conduct: float32 [16, 1024, 1024], P(None, 'gy', 'gx'), may hold values from 0.3 to 3
- excavated: int32 [16, 1024, 1024], P(None, 'gy', 'gx'), may hold values 0 or 1
- vectors_x: float32 [1024, 1024], replicated, may hold values from -0.1875 to 0.1875
- mass_x: float32 [1024], P('gy'), may hold values from 0.5 to 2
- values_x: float32 [1024], replicated, may hold values from 0.05 to 5
- vectors_y: float32 [1024, 1024], replicated, may hold values from -0.1875 to 0.1875
- mass_y: float32 [1024], P('gx'), may hold values from 0.5 to 2
- values_y: float32 [1024], replicated, may hold values from 0.05 to 5
- vertical_diag: float32 [16], replicated, may hold values from 3.2 to 4.5
- vertical_coupling: float32 [15], replicated, may hold values from 0.5 to 1.5
Outputs:
- adjoint: float32 [16, 1024, 1024], P(None, 'gy', 'gx')
- residual: float32 [16, 1024, 1024], P(None, 'gy', 'gx')
All inputs are finite; a program needn't handle non-finite values. No bound on the sum of `excavated` on one device may be relied on, other than what follows from the above.
Results may differ from a plain program's by a relative error of at most 0.0001.
Values sent between devices are 32-bit elements; how exact they have to be, the bound alone decides.
A program may use at most 128 MiB of HBM per device.

v0:
```python
import jax
import jax.numpy as jnp
from jax import lax
from jax.sharding import PartitionSpec as P

ITERS = 2


storage_term = 0.2


def padded_2(block, sides, width):
    for axis, dim in sides:
        count = lax.axis_size(axis)
        forward = [(i, i + 1) for i in range(count - 1)]
        backward = [(target, source) for source, target in forward]
        low = lax.ppermute(
            lax.slice_in_dim(block, block.shape[dim] - width, None, axis=dim), axis, forward
        )
        high = lax.ppermute(lax.slice_in_dim(block, 0, width, axis=dim), axis, backward)
        block = jnp.concatenate([low, block, high], axis=dim)
    return block


def harmonic(first, second):
    return 2.0 * first * second / (first + second)


def neighbours(padded):
    return [
        padded[2:, 1:-1, 1:-1],
        padded[:-2, 1:-1, 1:-1],
        padded[1:-1, 2:, 1:-1],
        padded[1:-1, :-2, 1:-1],
        padded[1:-1, 1:-1, 2:],
        padded[1:-1, 1:-1, :-2],
    ]


def faces_from(padded):
    center = padded[1:-1, 1:-1, 1:-1]
    return [harmonic(center, other) for other in neighbours(padded)]


def stencil(padded, faces):
    center = padded[1:-1, 1:-1, 1:-1]
    result = storage_term * center
    for face, other in zip(faces, neighbours(padded)):
        result = result + face * (center - other)
    return result


def pad_vertical(values):
    return jnp.pad(values, ((1, 1), (0, 0), (0, 0)))


def vertical_solve(rhs, diagonal, coupling, shifts):
    count = rhs.shape[0]
    ratios = []
    partial_value = []
    denom = diagonal[0] + shifts
    ratios.append(-coupling[0] / denom)
    partial_value.append(rhs[0] / denom)
    for position in range(1, count):
        denom = diagonal[position] + shifts + coupling[position - 1] * ratios[-1]
        if position < count - 1:
            ratios.append(-coupling[position] / denom)
        partial_value.append((rhs[position] + coupling[position - 1] * partial_value[-1]) / denom)
    solved = [partial_value[count - 1]]
    for position in range(count - 2, -1, -1):
        solved.append(partial_value[position] - ratios[position] * solved[-1])
    return jnp.stack(solved[::-1], axis=0)


def shards(
    right_side,
    conduct,
    excavated,
    vectors_x,
    mass_x,
    values_x,
    vectors_y,
    mass_y,
    values_y,
    vertical_diag,
    vertical_coupling,
):
    highest = lax.Precision.HIGHEST
    active = excavated.astype(jnp.float32)
    rim_conduct = padded_2(conduct, (("gy", 1), ("gx", 2)), 1)
    faces = faces_from(pad_vertical(rim_conduct))
    local_modes = right_side.shape[1] // lax.axis_size("gx")
    mode_start = (lax.axis_index("gx") * lax.axis_size("gy") + lax.axis_index("gy")) * local_modes
    local_values = lax.dynamic_slice_in_dim(values_x, mode_start, local_modes, 0)
    shifts = local_values[:, None] + values_y[None, :]
    adjoint = jnp.zeros_like(right_side)
    residual = right_side
    for iteration in range(ITERS):
        scaled = residual * mass_x[None, :, None] * mass_y[None, None, :]
        modes = jnp.einsum(
            "zxy,xi->ziy",
            lax.all_to_all(scaled, "gy", split_axis=0, concat_axis=1, tiled=True),
            vectors_x,
            precision=highest,
        )
        modes = lax.all_to_all(
            lax.all_to_all(modes, "gx", split_axis=1, concat_axis=2, tiled=True),
            "gy",
            split_axis=1,
            concat_axis=0,
            tiled=True,
        )
        modes = jnp.einsum("zxy,yj->zxj", modes, vectors_y, precision=highest)
        solved = vertical_solve(modes, vertical_diag, vertical_coupling, shifts)
        solved = jnp.einsum("zxj,yj->zxy", solved, vectors_y, precision=highest)
        solved = lax.all_to_all(
            lax.all_to_all(solved, "gy", split_axis=0, concat_axis=1, tiled=True),
            "gx",
            split_axis=2,
            concat_axis=1,
            tiled=True,
        )
        solved = jnp.einsum("ziy,xi->zxy", solved, vectors_x, precision=highest)
        update = lax.all_to_all(solved, "gy", split_axis=1, concat_axis=0, tiled=True)
        adjoint = adjoint + update
        masked = active * update
        rim_masked = padded_2(masked, (("gy", 1), ("gx", 2)), 1)
        image = stencil(pad_vertical(rim_masked), faces) + (1.0 - active) * update
        residual = residual - image
    return (adjoint, residual)


def solution(mesh):
    in_specs = (
        P(None, "gy", "gx"),
        P(None, "gy", "gx"),
        P(None, "gy", "gx"),
        P(),
        P("gy"),
        P(),
        P(),
        P("gx"),
        P(),
        P(),
        P(),
    )
    out_specs = (P(None, "gy", "gx"), P(None, "gy", "gx"))
    return jax.shard_map(shards, mesh=mesh, in_specs=in_specs, out_specs=out_specs, check_vma=False)
```

profile of v0, /device:TPU:0, one launch (start us, length us, event | category | flops | bytes accessed | tf_op | source)
XLA Modules:
  0.0 998.1 jit_solution(720027487343567933)
XLA Ops:
  3.9 55.2 %all_to_all.216 = f32[16,128,256]{1,2,0:T(8,128)S(1)} all-to-all(f32[16,128,256]{1,2,0:T(8,128)S(1)} %multiply_multiply_fusion.1), channel_id=1, replica_groups=mesh['gx'=4,'gy'=8] {'gy'}, dimensions={0} | all-to-all | bytes 4194304 | tf_op jit(solution)/shard_map/all_to_all | solution.py:102
  74.9 28.5 %all_to_all.217 = f32[2,1024,256]{2,0,1:T(2,128)S(1)} all-to-all(f32[2,1024,256]{2,0,1:T(2,128)S(1)} %copy.117), channel_id=1, replica_groups=mesh['gx'=4,'gy'=8] {'gx'}, dimensions={1} | all-to-all | bytes 4194304 | tf_op jit(solution)/shard_map/all_to_all | solution.py:107
  125.3 37.0 %all-to-all-done.2 = f32[2,256,1024]{2,0,1:T(2,128)S(1)} async-done(((f32[2,256,1024]{2,0,1:T(2,128)}), f32[2,256,1024]{2,0,1:T(2,128)S(1)}, u32[]{:S(2)}, u32[]{:S(2)}) %all-to-all-start.2) | async-done | bytes 2097184 | tf_op jit(solution)/shard_map/all_to_all | solution.py:106
  172.2 20.1 %subtract_dynamic-update-slice_fusion.1 = (f32[16,32,1024]{2,1,0:T(8,128)S(1)}, f32[1,32,1024]{2,1,0:T(8,128)S(1)}, f32[1,32,1024]{2,1,0:T(8,128)S(1)}, f32[1,32...) fusion(f32[]{:T(128)S(6)} %neg.60, ...), kind=kLoop, calls=%fused_computation.224 | loop fusion | flops 4521983 | bytes 3936568
  220.7 13.3 %constant_dynamic-update-slice_fusion.5 = f32[16,32,1024]{2,1,0:T(8,128)S(1)} fusion(f32[16,32,1024]{2,1,0:T(8,128)S(1)} %constant_dynamic-update-slice_fusion.6, f32[1,32,1024]{2,1,0:T(8,128)S(1)} %get-tuple-element.35, f32[1,32,1024]{2,1,0:T(8,128)S(1)} %get-tuple-element.32, f32[]{:T(128)} %bitcast.11, f32[]{:T(128)S(6)} %neg.60, f32[]{:T(128)} %bitcast.12, ...), kind=kLoop, calls=%fused_computation.257 | loop fusion | flops 1474560 | bytes 397952
  234.1 15.9 %constant_dynamic-update-slice_fusion.3 = f32[16,32,1024]{2,1,0:T(8,128)S(1)} fusion(f32[16,32,1024]{2,1,0:T(8,128)S(1)} %constant_dynamic-update-slice_fusion.4, f32[1,32,1024]{2,1,0:T(8,128)S(1)} %get-tuple-element.34, f32[1,32,1024]{2,1,0:T(8,128)S(1)} %get-tuple-element.33, f32[]{:T(128)} %bitcast.11, f32[]{:T(128)S(6)} %neg.60, f32[]{:T(128)} %bitcast.12, ...), kind=kLoop, calls=%fused_computation.255 | loop fusion | flops 1736704 | bytes 397976
  249.9 19.8 %constant_dynamic-update-slice_fusion.1 = f32[16,32,1024]{2,1,0:T(8,128)S(1)} fusion(f32[16,32,1024]{2,1,0:T(8,128)S(1)} %constant_dynamic-update-slice_fusion.2, f32[]{:T(128)} %bitcast.11, f32[]{:T(128)S(6)} %neg.60, f32[]{:T(128)} %bitcast.12, f32[]{:T(128)} %bitcast.13, f32[]{:T(128)S(6)} %neg.61, f32[]{:T(128)} %bitcast.14, f32[]{:T(128)} %bitcast.15, ...), kind=kLoop, calls=%fused_computation.253 | loop fusion | flops 2392064 | bytes 660152
  269.7 19.8 %constant_dynamic-update-slice_fusion = f32[16,32,1024]{2,1,0:T(8,128)S(1)} fusion(f32[16,32,1024]{2,1,0:T(8,128)S(1)} %constant_dynamic-update-slice_fusion.1, f32[]{:T(128)} %bitcast.11, f32[]{:T(128)S(6)} %neg.60, f32[]{:T(128)} %bitcast.12, f32[]{:T(128)} %bitcast.13, f32[]{:T(128)S(6)} %neg.61, f32[]{:T(128)} %bitcast.14, f32[]{:T(128)} %bitcast.15, ...), kind=kLoop, calls=%fused_computation.252 | loop fusion | flops 2326528 | bytes 660152 | tf_op jit(solution)/shard_map/stack | solution.py:72
  296.7 51.5 %all_to_all.218 = f32[16,32,1024]{2,1,0:T(8,128)S(1)} all-to-all(f32[16,32,1024]{2,1,0:T(8,128)S(1)} %fusion.5), channel_id=1, replica_groups=mesh['gx'=4,'gy'=8] {'gy'}, dimensions={0} | all-to-all | bytes 4194304 | tf_op jit(solution)/shard_map/all_to_all | solution.py:117
  350.8 29.1 %all_to_all.219 = f32[2,256,1024]{1,0,2:T(2,128)S(1)} all-to-all(f32[2,256,1024]{1,0,2:T(2,128)} %copy.124), channel_id=1, replica_groups=mesh['gx'=4,'gy'=8] {'gx'}, dimensions={2} | all-to-all | bytes 4194304 | tf_op jit(solution)/shard_map/all_to_all | solution.py:116
  410.2 33.9 %all-to-all-done.5 = f32[2,1024,256]{2,0,1:T(2,128)S(1)} async-done(((f32[2,1024,256]{2,0,1:T(2,128)}), f32[2,1024,256]{2,0,1:T(2,128)S(1)}, u32[]{:S(2)}, u32[]{:S(2)}) %all-to-all-start.5) | async-done | bytes 2097184 | tf_op jit(solution)/shard_map/all_to_all | solution.py:124
  489.7 15.2 %multiply_multiply_fusion = (f32[16,128,256]{1,2,0:T(8,128)}, f32[16,128,256]{1,2,0:T(8,128)}, f32[16,128,256]{1,2,0:T(8,128)}, f32[16,128,256]{1,2,0:T(8,128)}) fusion(f32[256]{0:T(256)S(1)} %copy-done.20, f32[128]{0:T(128)S(1)} %copy-done.21, f32[16,128,256]{1,2,0:T(8,128)} %copy-done.16, f32[2,8,128,256]{2,3,0,1:T(8,128)} %copy.128, ...), kind=kLoop, calls=%fused_computation.102 | loop fusion | flops 31981568 | bytes 27363328 | tf_op jit(solution)/shard_map/mul | solution.py:99
  504.9 55.4 %all_to_all.220 = f32[16,128,256]{1,2,0:T(8,128)S(1)} all-to-all(f32[16,128,256]{1,2,0:T(8,128)} %get-tuple-element.22), channel_id=1, replica_groups=mesh['gx'=4,'gy'=8] {'gy'}, dimensions={0} | all-to-all | bytes 4194304 | tf_op jit(solution)/shard_map/all_to_all | solution.py:102
  576.2 29.2 %all_to_all.221 = f32[2,1024,256]{2,0,1:T(2,128)S(1)} all-to-all(f32[2,1024,256]{2,0,1:T(2,128)S(1)} %copy.166), channel_id=1, replica_groups=mesh['gx'=4,'gy'=8] {'gx'}, dimensions={1} | all-to-all | bytes 4194304 | tf_op jit(solution)/shard_map/all_to_all | solution.py:107
  610.2 52.0 %all_to_all.222 = f32[2,256,1024]{2,0,1:T(2,128)S(1)} all-to-all(f32[2,256,1024]{2,0,1:T(2,128)S(1)} %copy.169), channel_id=1, replica_groups=mesh['gx'=4,'gy'=8] {'gy'}, dimensions={1} | all-to-all | bytes 4194304 | tf_op jit(solution)/shard_map/all_to_all | solution.py:106
  672.0 20.1 %subtract_dynamic-update-slice_fusion = (f32[16,32,1024]{2,1,0:T(8,128)S(1)}, f32[1,32,1024]{2,1,0:T(8,128)S(1)}, f32[1,32,1024]{2,1,0:T(8,128)S(1)}, f32[1,32,1...) fusion(f32[]{:T(128)S(6)} %neg.60, ...), kind=kLoop, calls=%fused_computation.209 | loop fusion | flops 4521983 | bytes 3936568
  720.6 13.3 %constant_dynamic-update-slice_fusion.20 = f32[16,32,1024]{2,1,0:T(8,128)S(1)} fusion(f32[16,32,1024]{2,1,0:T(8,128)S(1)} %constant_dynamic-update-slice_fusion.21, f32[1,32,1024]{2,1,0:T(8,128)S(1)} %get-tuple-element.17, f32[1,32,1024]{2,1,0:T(8,128)S(1)} %get-tuple-element.14, f32[]{:T(128)} %bitcast.11, f32[]{:T(128)S(6)} %neg.60, f32[]{:T(128)} %bitcast.12, ...), kind=kLoop, calls=%fused_computation.272 | loop fusion | flops 1474560 | bytes 397952
  733.9 15.9 %constant_dynamic-update-slice_fusion.18 = f32[16,32,1024]{2,1,0:T(8,128)S(1)} fusion(f32[16,32,1024]{2,1,0:T(8,128)S(1)} %constant_dynamic-update-slice_fusion.19, f32[1,32,1024]{2,1,0:T(8,128)S(1)} %get-tuple-element.16, f32[1,32,1024]{2,1,0:T(8,128)S(1)} %get-tuple-element.15, f32[]{:T(128)} %bitcast.11, f32[]{:T(128)S(6)} %neg.60, f32[]{:T(128)} %bitcast.12, ...), kind=kLoop, calls=%fused_computation.270 | loop fusion | flops 1736704 | bytes 397976
  749.8 19.8 %constant_dynamic-update-slice_fusion.16 = f32[16,32,1024]{2,1,0:T(8,128)S(1)} fusion(f32[16,32,1024]{2,1,0:T(8,128)S(1)} %constant_dynamic-update-slice_fusion.17, f32[]{:T(128)} %bitcast.11, f32[]{:T(128)S(6)} %neg.60, f32[]{:T(128)} %bitcast.12, f32[]{:T(128)} %bitcast.13, f32[]{:T(128)S(6)} %neg.61, f32[]{:T(128)} %bitcast.14, f32[]{:T(128)} %bitcast.15, ...), kind=kLoop, calls=%fused_computation.268 | loop fusion | flops 2392064 | bytes 660152
  769.6 19.8 %constant_dynamic-update-slice_fusion.15 = f32[16,32,1024]{2,1,0:T(8,128)S(1)} fusion(f32[16,32,1024]{2,1,0:T(8,128)S(1)} %constant_dynamic-update-slice_fusion.16, f32[]{:T(128)} %bitcast.11, f32[]{:T(128)S(6)} %neg.60, f32[]{:T(128)} %bitcast.12, f32[]{:T(128)} %bitcast.13, f32[]{:T(128)S(6)} %neg.61, f32[]{:T(128)} %bitcast.14, f32[]{:T(128)} %bitcast.15, ...), kind=kLoop, calls=%fused_computation.267 | loop fusion | flops 2326528 | bytes 660152 | tf_op jit(solution)/shard_map/stack | solution.py:72
  796.6 51.5 %all_to_all.223 = f32[16,32,1024]{2,1,0:T(8,128)S(1)} all-to-all(f32[16,32,1024]{2,1,0:T(8,128)S(1)} %fusion.1), channel_id=1, replica_groups=mesh['gx'=4,'gy'=8] {'gy'}, dimensions={0} | all-to-all | bytes 4194304 | tf_op jit(solution)/shard_map/all_to_all | solution.py:117
  850.7 29.1 %all_to_all.224 = f32[2,256,1024]{1,0,2:T(2,128)S(1)} all-to-all(f32[2,256,1024]{1,0,2:T(2,128)} %copy.173), channel_id=1, replica_groups=mesh['gx'=4,'gy'=8] {'gx'}, dimensions={2} | all-to-all | bytes 4194304 | tf_op jit(solution)/shard_map/all_to_all | solution.py:116
  893.3 52.2 %all_to_all.225 = f32[2,1024,256]{2,0,1:T(2,128)} all-to-all(f32[2,1024,256]{2,0,1:T(2,128)S(1)} %copy.176), channel_id=1, replica_groups=mesh['gx'=4,'gy'=8] {'gy'}, dimensions={1} | all-to-all | bytes 4194304 | tf_op jit(solution)/shard_map/all_to_all | solution.py:124
  983.2 11.6 %fusion.21 = f32[16,128,256]{1,2,0:T(8,128)} fusion(f32[16,128,256]{1,2,0:T(8,128)} %get-tuple-element.23, f32[16,128,256]{1,2,0:T(8,128)} %get-tuple-element.25, f32[16,128,256]{1,2,0:T(8,128)S(1)} %get-tuple-element.48, f32[16,130,1]{1,2,0:T(1,128)S(1)} %copy.184, f32[16,1,256]{1,2,0:T(8,128)} %copy.181, f32[16,1,256]{1,2,0:T(8,128)S(1)} %copy-done.13, ...), kind=kLoop, calls=%fused_computation.36 | loop fusion | flops 24641536 | bytes 25248000 | tf_op jit(solution)/shard_map/sub | solution.py:129
  (172 shorter events, 277.8 us)
Async XLA Ops:
  109.6 15.0 %copy-start.18 = (f32[16]{0:T(128)S(1)}, f32[16]{0:T(128)}, u32[]{:S(2)}) copy-start(f32[16]{0:T(128)} %param.20) | copy-start | bytes 196
  109.6 52.7 %all-to-all-start.2 = ((f32[2,256,1024]{2,0,1:T(2,128)}), f32[2,256,1024]{2,0,1:T(2,128)S(1)}, u32[]{:S(2)}, u32[]{:S(2)}) async-start(f32[2,256,1024]{2,0,1:T(2,128)} %copy.120), calls=%async_computation.2 | async-start | bytes 4194304 | tf_op jit(solution)/shard_map/all_to_all | solution.py:106
  165.2 6.9 copy-start.17
  391.5 52.6 %all-to-all-start.5 = ((f32[2,1024,256]{2,0,1:T(2,128)}), f32[2,1024,256]{2,0,1:T(2,128)S(1)}, u32[]{:S(2)}, u32[]{:S(2)}) async-start(f32[2,1024,256]{2,0,1:T(2,128)} %copy.127), calls=%async_computation.5 | async-start | bytes 4194304 | tf_op jit(solution)/shard_map/all_to_all | solution.py:124
  396.1 10.2 %collective-permute-start.1 = (f32[16,1,256]{2,0,1:T(8,128)S(1)}, f32[16,1,256]{2,0,1:T(8,128)S(1)}, u32[]{:S(2)}, u32[]{:S(2)}) collective-permute-start(f32[16,1,256]{2,0,1:T(8,128)S(1)} %copy.193), channel_id=1, source_target_pairs={{1,0},{2,1},{3,2},{4,3},{5,4},{6,5},{7,6},{9,8},{10,9},{11,10},{12... | collective-permute-start | bytes 49160 | tf_op jit(solution)/shard_map/ppermute | solution.py:20
  397.4 10.8 %collective-permute-start = (f32[16,1,256]{2,0,1:T(8,128)S(1)}, f32[16,1,256]{2,0,1:T(8,128)S(1)}, u32[]{:S(2)}, u32[]{:S(2)}) collective-permute-start(f32[16,1,256]{2,0,1:T(8,128)S(1)} %copy.192), channel_id=1, source_target_pairs={{0,1},{1,2},{2,3},{3,4},{4,5},{5,6},{6,7},{8,9},{9,10},{10,11},{11... | collective-permute-start | bytes 49160 | tf_op jit(solution)/shard_map/ppermute | solution.py:17
  455.9 14.8 %collective-permute-start.5 = (f32[16,1,256]{2,0,1:T(8,128)S(1)}, f32[16,1,256]{2,0,1:T(8,128)S(1)}, u32[]{:S(2)}, u32[]{:S(2)}) collective-permute-start(f32[16,1,256]{2,0,1:T(8,128)S(1)} %copy.142), channel_id=1, source_target_pairs={{1,0},{2,1},{3,2},{4,3},{5,4},{6,5},{7,6},{9,8},{10,9},{11,10},{12... | collective-permute-start | bytes 49160 | tf_op jit(solution)/shard_map/ppermute | solution.py:20
  457.2 11.5 %collective-permute-start.4 = (f32[16,1,256]{2,0,1:T(8,128)S(1)}, f32[16,1,256]{2,0,1:T(8,128)S(1)}, u32[]{:S(2)}, u32[]{:S(2)}) collective-permute-start(f32[16,1,256]{2,0,1:T(8,128)S(1)} %copy.141), channel_id=1, source_target_pairs={{0,1},{1,2},{2,3},{3,4},{4,5},{5,6},{6,7},{8,9},{9,10},{10,11},{11... | collective-permute-start | bytes 49160 | tf_op jit(solution)/shard_map/ppermute | solution.py:17
  461.5 6.3 collective-permute-start.3
  462.8 6.0 collective-permute-start.2
  472.8 7.1 copy-start.6
  472.8 7.1 copy-start.8
  472.8 7.1 copy-start.10
  474.0 10.9 %copy-start.14 = (f32[16,1,256]{1,2,0:T(8,128)S(1)}, f32[16,1,256]{1,2,0:T(8,128)}, u32[]{:S(2)}) copy-start(f32[16,1,256]{1,2,0:T(8,128)} %copy.143) | copy-start | bytes 49156
  474.1 10.9 %copy-start.15 = (f32[16,1,256]{1,2,0:T(8,128)S(1)}, f32[16,1,256]{1,2,0:T(8,128)}, u32[]{:S(2)}) copy-start(f32[16,1,256]{1,2,0:T(8,128)} %copy.144) | copy-start | bytes 49156
  474.1 9.0 collective-permute-start.6
  478.5 6.4 collective-permute-start.7
  483.1 6.6 copy-start.12
  959.3 4.9 collective-permute-start.8
  962.9 3.4 collective-permute-start.9
  969.3 7.3 collective-permute-start.10
  972.2 5.6 collective-permute-start.11
  977.9 5.0 copy-start.5
  977.9 5.3 copy-start.13
  (12 other events, 38.2 us)
where the time goes:
time: 1010 us; the launch traced here: 998 us
  blocking collectives  434 us (43%)
  other arithmetic  285 us (28%)
  local copies, waits for them, and re-layouts  94.1 us (9%)
  waiting for transfers between devices  74.8 us (7%)
  matrix products  63.9 us (6%)
  starting transfers between devices  35.3 us (3%)
  between operations  11.3 us (1%)
    unnamed x16, other arithmetic  195 us
    all_to_all x2, blocking collectives, shards(): lax.all_to_all(scaled, 'gy', split_axis=0, concat_axis=1, tiled=True)  111 us
    all_to_all x2, blocking collectives, shards(): lax.all_to_all(solved, 'gy', split_axis=0, concat_axis=1, tiled=True)  103 us
    all_to_all x2, blocking collectives, shards(): lax.all_to_all(lax.all_to_all(solved, 'gy', split_axis=0, concat_axis=1,...  58.2 us
    all_to_all x2, blocking collectives, shards(): lax.all_to_all(modes, 'gx', split_axis=1, concat_axis=2, tiled=True)  57.7 us
    all_to_all x1, blocking collectives, shards(): lax.all_to_all(solved, 'gy', split_axis=1, concat_axis=0, tiled=True)  52.2 us
    all_to_all x1, blocking collectives, shards(): lax.all_to_all(lax.all_to_all(modes, 'gx', split_axis=1, concat_axis=2, t...  52 us
    another operation x2, other arithmetic, vertical_solve(): return jnp.stack(solved[::-1], axis=0)  39.5 us
  transfers between devices with their start and end apart: 14, of which 5 were waited for; matrix products, arithmetic and copies ran while one was open for 3% of the time, Pallas kernels for 0%

commit v1 on v0

v1 whole, which is shorter than its diff:
```python
import functools
import jax
import jax.numpy as jnp
from jax import lax
from jax.experimental import pallas as pl
from jax.experimental.pallas import tpu as pltpu
from jax.sharding import PartitionSpec as P

ITERS = 2
LANES = 128
VMEM = pltpu.VMEM

storage_term = 0.2


def padded_2(block, sides, width):
    for axis, dim in sides:
        count = lax.axis_size(axis)
        forward = [(i, i + 1) for i in range(count - 1)]
        backward = [(target, source) for source, target in forward]
        low = lax.ppermute(
            lax.slice_in_dim(block, block.shape[dim] - width, None, axis=dim), axis, forward
        )
        high = lax.ppermute(lax.slice_in_dim(block, 0, width, axis=dim), axis, backward)
        block = jnp.concatenate([low, block, high], axis=dim)
    return block


def harmonic(first, second):
    return 2.0 * first * second / (first + second)


def neighbours(padded):
    return [
        padded[2:, 1:-1, 1:-1],
        padded[:-2, 1:-1, 1:-1],
        padded[1:-1, 2:, 1:-1],
        padded[1:-1, :-2, 1:-1],
        padded[1:-1, 1:-1, 2:],
        padded[1:-1, 1:-1, :-2],
    ]


def faces_from(padded):
    center = padded[1:-1, 1:-1, 1:-1]
    return [harmonic(center, other) for other in neighbours(padded)]


def stencil(padded, faces):
    center = padded[1:-1, 1:-1, 1:-1]
    result = storage_term * center
    for face, other in zip(faces, neighbours(padded)):
        result = result + face * (center - other)
    return result


def pad_vertical(values):
    return jnp.pad(values, ((1, 1), (0, 0), (0, 0)))


def split(value):
    high = value.astype(jnp.bfloat16)
    return high, (value - high.astype(jnp.float32)).astype(jnp.bfloat16)


def dot3(first, second, dims):
    def one(a, b):
        return lax.dot_general(a, b, (dims, ((), ())), preferred_element_type=jnp.float32)

    return one(first[0], second[0]) + (one(first[0], second[1]) + one(first[1], second[0]))


def split_kernel(in_ref, high_ref, low_ref):
    high_ref[...], low_ref[...] = split(in_ref[...])


def split_matrix(matrix):
    rows, columns = matrix.shape
    spec = pl.BlockSpec((rows // 8, columns), lambda i: (i, 0))
    return pl.pallas_call(
        split_kernel,
        grid=(8,),
        out_shape=[jax.ShapeDtypeStruct(matrix.shape, jnp.bfloat16)] * 2,
        in_specs=[spec],
        out_specs=[spec, spec],
    )(matrix)


def forward_y_kernel(in_ref, high_ref, low_ref, out_ref, low_in, high_in):
    sources, count, part = in_ref.shape
    for source in range(sources):
        high, low = split(in_ref[source])
        high_in[:, source * part : (source + 1) * part] = high
        low_in[:, source * part : (source + 1) * part] = low
    modes = high_ref.shape[1]
    width = 256

    @pl.loop(0, modes // width)
    def _(step):
        columns = pl.ds(pl.multiple_of(step * width, width), width)
        out_ref[columns, :] = dot3(
            (high_ref[:, columns], low_ref[:, columns]),
            (high_in[...], low_in[...]),
            ((0,), (1,)),
        )


def forward_y(values, high, low):
    sources, count, part = values.shape
    size = sources * part
    return pl.pallas_call(
        forward_y_kernel,
        out_shape=jax.ShapeDtypeStruct((size, count), jnp.float32),
        in_specs=[pl.BlockSpec(memory_space=VMEM)] * 3,
        out_specs=pl.BlockSpec(memory_space=VMEM),
        scratch_shapes=[VMEM((count, size), jnp.bfloat16)] * 2,
        compiler_params=pltpu.CompilerParams(vmem_limit_bytes=48 << 20),
    )(values, high, low)


def inverse_y_kernel(in_ref, high_ref, low_ref, out_ref, high_in, low_in):
    targets, count, part = out_ref.shape
    moved = jnp.transpose(in_ref[...])
    high_in[...], low_in[...] = split(moved)
    for target in range(targets):
        rows = slice(target * part, (target + 1) * part)
        out_ref[target] = dot3(
            (high_in[...], low_in[...]), (high_ref[rows, :], low_ref[rows, :]), ((1,), (1,))
        )


def inverse_y(values, high, low, targets):
    size, count = values.shape
    return pl.pallas_call(
        inverse_y_kernel,
        out_shape=jax.ShapeDtypeStruct((targets, count, size // targets), jnp.float32),
        in_specs=[pl.BlockSpec(memory_space=VMEM)] * 3,
        out_specs=pl.BlockSpec(memory_space=VMEM),
        scratch_shapes=[VMEM((count, size), jnp.bfloat16)] * 2,
        compiler_params=pltpu.CompilerParams(vmem_limit_bytes=48 << 20),
    )(values, high, low)


def swap_blocks(tiles, part):
    count = len(tiles)
    lane = lax.broadcasted_iota(jnp.int32, tiles[0].shape, 1) // part
    result = []
    for a in range(count):
        made = None
        for b in range(count):
            shift = ((b - a) * part) % LANES
            moved = pltpu.roll(tiles[b], shift, 1) if shift else tiles[b]
            made = moved if made is None else jnp.where(lane == b, moved, made)
        result.append(made)
    return result


def middle_kernel(
    in_ref, high_ref, low_ref, values_x_ref, values_y_ref, diag_ref, coup_ref, out_ref,
    high_in, low_in, work, ratios,
):
    devices, modes, packed = in_ref.shape
    levels = diag_ref.shape[0]
    part = packed // levels
    group = LANES // part
    size = devices * part
    for tile in range(packed // LANES):
        lanes = slice(tile * LANES, (tile + 1) * LANES)

        @pl.loop(0, devices // group)
        def _(g):
            tiles = [in_ref[g * group + b, :, lanes] for b in range(group)]
            columns = pl.ds(pl.multiple_of(g * LANES, LANES), LANES)
            for a, made in enumerate(swap_blocks(tiles, part)):
                rows = slice((tile * group + a) * modes, (tile * group + a + 1) * modes)
                work[rows, columns] = made

    high_in[...], low_in[...] = split(work[...])
    width = 256

    @pl.loop(0, size // width)
    def _(step):
        columns = pl.ds(pl.multiple_of(step * width, width), width)
        work[:, columns] = dot3(
            (high_in[...], low_in[...]), (high_ref[:, columns], low_ref[:, columns]), ((1,), (0,))
        )

    wide = 512

    @pl.loop(0, size // wide)
    def _(step):
        columns = pl.ds(pl.multiple_of(step * wide, wide), wide)
        for start in range(0, modes, 8):
            shifts = values_x_ref[:, columns] + values_y_ref[start : start + 8, :]
            ratio = partial = None
            for z in range(levels):
                rows = slice(z * modes + start, z * modes + start + 8)
                denom = diag_ref[z] + shifts
                rhs = work[rows, columns]
                if z:
                    denom = denom + coup_ref[z - 1] * ratio
                    rhs = rhs + coup_ref[z - 1] * partial
                inverse = 1.0 / denom
                partial = rhs * inverse
                work[rows, columns] = partial
                if z < levels - 1:
                    ratio = -coup_ref[z] * inverse
                    ratios[rows, columns] = ratio
            solved = partial
            for z in range(levels - 1, -1, -1):
                rows = slice(z * modes + start, z * modes + start + 8)
                if z < levels - 1:
                    solved = work[rows, columns] - ratios[rows, columns] * solved
                work[rows, columns] = solved

    high_in[...], low_in[...] = split(work[...])

    @pl.loop(0, size // width)
    def _(step):
        rows = pl.ds(pl.multiple_of(step * width, width), width)
        work[:, rows] = dot3(
            (high_in[...], low_in[...]), (high_ref[rows, :], low_ref[rows, :]), ((1,), (1,))
        )

    for tile in range(packed // LANES):
        lanes = slice(tile * LANES, (tile + 1) * LANES)

        @pl.loop(0, devices // group)
        def _(g):
            columns = pl.ds(pl.multiple_of(g * LANES, LANES), LANES)
            tiles = [
                work[(tile * group + a) * modes : (tile * group + a + 1) * modes, columns]
                for a in range(group)
            ]
            for b, made in enumerate(swap_blocks(tiles, part)):
                out_ref[g * group + b, :, lanes] = made


def middle(values, high, low, values_x, values_y, diag, coup):
    devices, modes, packed = values.shape
    size = high.shape[0]
    count = modes * diag.shape[0]
    vmem = pl.BlockSpec(memory_space=VMEM)
    smem = pl.BlockSpec(memory_space=pltpu.SMEM)
    return pl.pallas_call(
        middle_kernel,
        out_shape=jax.ShapeDtypeStruct(values.shape, jnp.float32),
        in_specs=[vmem] * 5 + [smem] * 2,
        out_specs=vmem,
        scratch_shapes=[VMEM((count, size), jnp.bfloat16)] * 2
        + [VMEM((count, size), jnp.float32)] * 2,
        compiler_params=pltpu.CompilerParams(vmem_limit_bytes=48 << 20),
    )(values, high, low, values_x[None, :], values_y[:, None], diag, coup)


def shards(
    right_side,
    conduct,
    excavated,
    vectors_x,
    mass_x,
    values_x,
    vectors_y,
    mass_y,
    values_y,
    vertical_diag,
    vertical_coupling,
):
    columns, lines = lax.axis_size("gx"), lax.axis_size("gy")
    devices = columns * lines
    levels, rows, part_y = right_side.shape
    part_x = rows // columns
    modes = vectors_y.shape[1] // devices
    both = ("gy", "gx")
    active = excavated.astype(jnp.float32)
    rim_conduct = padded_2(conduct, (("gy", 1), ("gx", 2)), 1)
    faces = faces_from(pad_vertical(rim_conduct))
    high_x, low_x = split_matrix(vectors_x)
    high_y, low_y = split_matrix(vectors_y)
    start = (lax.axis_index("gy") * columns + lax.axis_index("gx")) * modes
    local_values = lax.dynamic_slice_in_dim(values_y, start, modes, 0)
    adjoint = jnp.zeros_like(right_side)
    residual = right_side
    for iteration in range(ITERS):
        scaled = residual * mass_x[None, :, None] * mass_y[None, None, :]
        scaled = scaled.reshape(levels, columns, part_x, part_y).transpose(1, 0, 2, 3)
        scaled = scaled.reshape(columns, levels * part_x, part_y)
        got = lax.all_to_all(scaled, "gx", split_axis=0, concat_axis=0, tiled=True)
        lines_y = forward_y(got, high_y, low_y)
        lines_y = lines_y.reshape(devices, modes, levels * part_x)
        got = lax.all_to_all(lines_y, both, split_axis=0, concat_axis=0, tiled=True)
        solved = middle(
            got, high_x, low_x, values_x, local_values, vertical_diag, vertical_coupling
        )
        got = lax.all_to_all(solved, both, split_axis=0, concat_axis=0, tiled=True)
        got = got.reshape(devices * modes, levels * part_x)
        back = inverse_y(got, high_y, low_y, columns)
        back = lax.all_to_all(back, "gx", split_axis=0, concat_axis=0, tiled=True)
        back = back.reshape(columns, levels, part_x, part_y).transpose(1, 0, 2, 3)
        update = back.reshape(levels, rows, part_y)
        adjoint = adjoint + update
        masked = active * update
        rim_masked = padded_2(masked, (("gy", 1), ("gx", 2)), 1)
        image = stencil(pad_vertical(rim_masked), faces) + (1.0 - active) * update
        residual = residual - image
    return (adjoint, residual)


def solution(mesh):
    in_specs = (
        P(None, "gy", "gx"),
        P(None, "gy", "gx"),
        P(None, "gy", "gx"),
        P(),
        P("gy"),
        P(),
        P(),
        P("gx"),
        P(),
        P(),
        P(),
    )
    out_specs = (P(None, "gy", "gx"), P(None, "gy", "gx"))
    return jax.shard_map(shards, mesh=mesh, in_specs=in_specs, out_specs=out_specs, check_vma=False)
```

time: 1010 us -> 498 us (0.49)
  other arithmetic: 285 us -> 44 us
  blocking collectives: 434 us -> 216 us
  Pallas kernels: 0 us -> 78.4 us
  matrix products: 63.9 us -> 0 us
  local copies, waits for them, and re-layouts: 94.1 us -> 30.8 us
  between operations: 11.3 us -> 1.02 us
    all_to_all x10 -> x5, blocking collectives: 434 us -> 216 us  [the longest x2 105 us: shards(): got = lax.all_to_all(solved, both, split_axis=0, concat_axis=0, tiled=True)]
    unnamed x16 -> x0, other arithmetic: 195 us -> none
    pallas_call x0 -> x8, Pallas kernels: none -> 78.4 us  [the longest x2 38.8 us: middle(): pl.pallas_call(middle_kernel, out_shape=jax.ShapeDtypeStruct(values.shape...]
    dot_general x8 -> x0, matrix products: 63.9 us -> none  [the longest x2 20.5 us: shards(): jnp.einsum('zxy,xi->ziy', lax.all_to_all(scaled, 'gy', split_axis=0, conc...]
    another operation x2 -> x0, other arithmetic: 39.5 us -> none  [vertical_solve(): return jnp.stack(solved[::-1], axis=0)]
    all_to_all x24 -> x0, local copies, waits for them, and re-layouts: 30.8 us -> none  [the longest x6 11.1 us: shards(): lax.all_to_all(modes, 'gx', split_axis=1, concat_axis=2, tiled=True)]
    unnamed x65 -> x44, local copies, waits for them, and re-layouts: 22.9 us -> 4.29 us
    all_to_all x2 -> x3, waiting for transfers between devices: 70.9 us -> 77.2 us  [the longest x1 41.8 us: shards(): got = lax.all_to_all(lines_y, both, split_axis=0, concat_axis=0, tiled=True)]
  transfers between devices with their start and end apart: 14 -> 15, of which waited for: 5 -> 7; matrix products, arithmetic and copies ran while one was open for 3% -> 4% of each run, Pallas kernels for 0% -> 3%
where the time goes in v1:
time: 498 us; the launch traced here: 495 us
  blocking collectives  216 us (43%)
  waiting for transfers between devices  84.8 us (17%)
  Pallas kernels  78.4 us (16%)
  other arithmetic  44 us (9%)
  starting transfers between devices  40.5 us (8%)
  local copies, waits for them, and re-layouts  30.8 us (6%)
    all_to_all x2, blocking collectives, shards(): got = lax.all_to_all(solved, both, split_axis=0, concat_axis=0, tiled=True)  105 us
    all_to_all x1, blocking collectives, shards(): got = lax.all_to_all(lines_y, both, split_axis=0, concat_axis=0, tiled=True)  50.7 us
    all_to_all x1, waiting for transfers between devices, shards(): got = lax.all_to_all(lines_y, both, split_axis=0, concat_axis=0, tiled=True)  41.8 us
    pallas_call x2, Pallas kernels, middle(): pl.pallas_call(middle_kernel, out_shape=jax.ShapeDtypeStruct(values.shape...  38.8 us
    all_to_all x1, blocking collectives, shards(): got = lax.all_to_all(scaled, 'gx', split_axis=0, concat_axis=0, tiled=True)  31.8 us
    all_to_all x1, blocking collectives, shards(): back = lax.all_to_all(back, 'gx', split_axis=0, concat_axis=0, tiled=True)  28.3 us
    all_to_all x1, waiting for transfers between devices, shards(): got = lax.all_to_all(scaled, 'gx', split_axis=0, concat_axis=0, tiled=True)  18.2 us
    ppermute x6, starting transfers between devices, padded_2(): lax.ppermute(lax.slice_in_dim(block, block.shape[dim] - width, None, axis...  17.8 us
  transfers between devices with their start and end apart: 15, of which 7 were waited for; matrix products, arithmetic and copies ran while one was open for 4% of the time, Pallas kernels for 3%

profile of v1, /device:TPU:0, one launch (start us, length us, event | category | flops | bytes accessed | tf_op | source)
XLA Modules:
  0.0 495.4 jit_solution(4690611374206926571)
XLA Ops:
  4.0 5.2 %all-to-all-start = ((f32[4,512,256]{2,1,0:T(8,128)}), f32[4,512,256]{2,1,0:T(8,128)S(1)}, u32[]{:S(2)}, u32[]{:S(2)}) async-start(f32[4,512,256]{2,1,0:T(8,128)} %bitcast.42), calls=%async_computation | async-start | bytes 4194304 | tf_op jit(solution)/shard_map/all_to_all | solution.py:288
  9.2 6.6 %shard_map.122 = (bf16[1024,1024]{1,0:T(8,128)(2,1)}, bf16[1024,1024]{1,0:T(8,128)(2,1)}) custom-call(f32[1024,1024]{1,0:T(8,128)} %in_ref.2), custom_call_target="tpu_custom_call" | custom-call | tf_op jit(solution)/shard_map/pallas_call | solution.py:80
  15.8 18.2 %all-to-all-done.in_ref = f32[4,512,256]{2,1,0:T(8,128)S(1)} async-done(((f32[4,512,256]{2,1,0:T(8,128)}), f32[4,512,256]{2,1,0:T(8,128)S(1)}, u32[]{:S(2)}, u32[]{:S(2)}) %all-to-all-start) | async-done | bytes 2097184 | tf_op jit(solution)/shard_map/all_to_all | solution.py:288
  34.0 6.7 %shard_map.123 = f32[1024,512]{1,0:T(8,128)S(1)} custom-call(f32[4,512,256]{2,1,0:T(8,128)S(1)} %all-to-all-done.in_ref, bf16[1024,1024]{1,0:T(8,128)(2,1)} %get-tuple-element.6.high_ref, bf16[1024,1024]{1,0:T(8,128)(2,1)} %get-tuple-element.7.low_ref), custom_call_target="tpu_custom_call" | custom-call | tf_op jit(solution)/shard_map/pallas_call | solution.py:111
  42.1 5.0 %all-to-all-start.1 = ((f32[32,32,512]{2,1,0:T(8,128)}), f32[32,32,512]{2,1,0:T(8,128)S(1)}, u32[]{:S(2)}, u32[]{:S(2)}) async-start(f32[32,32,512]{2,1,0:T(8,128)} %bitcast.34), calls=%async_computation.1 | async-start | bytes 4194304 | tf_op jit(solution)/shard_map/all_to_all | solution.py:291
  47.3 6.7 %shard_map.124 = (bf16[1024,1024]{1,0:T(8,128)(2,1)}, bf16[1024,1024]{1,0:T(8,128)(2,1)}) custom-call(f32[1024,1024]{1,0:T(8,128)} %in_ref.3), custom_call_target="tpu_custom_call" | custom-call | tf_op jit(solution)/shard_map/pallas_call | solution.py:80
  54.1 41.8 %all-to-all-done.1.in_ref = f32[32,32,512]{2,1,0:T(8,128)S(1)} async-done(((f32[32,32,512]{2,1,0:T(8,128)}), f32[32,32,512]{2,1,0:T(8,128)S(1)}, u32[]{:S(2)}, u32[]{:S(2)}) %all-to-all-start.1) | async-done | bytes 2097184 | tf_op jit(solution)/shard_map/all_to_all | solution.py:291
  95.9 19.4 %shard_map.125 = f32[32,32,512]{2,1,0:T(8,128)S(1)} custom-call(f32[32,32,512]{2,1,0:T(8,128)S(1)} %all-to-all-done.1.in_ref, bf16[1024,1024]{1,0:T(8,128)(2,1)} %get-tuple-element.8.high_ref, bf16[1024,1024]{1,0:T(8,128)(2,1)} %get-tuple-element.9.low_ref, f32[1,1024]{1,0:T(1,128)S(1)} %bitcast.38, f32[32,1]{1,0:T(8,128)S(1)} %copy.43.values_y_ref, ...), custom_call_target="tpu_custom_call" | custom-call | tf_op jit(solution)/shard_map/pallas_call | solution.py:245
  115.3 53.1 %all_to_all.40 = f32[32,32,512]{2,1,0:T(8,128)S(1)} all-to-all(f32[32,32,512]{2,1,0:T(8,128)S(1)} %shard_map.125), channel_id=1, replica_groups=mesh['gx'=4,'gy'=8] {'gy','gx'}, dimensions={0} | all-to-all | bytes 4194304 | tf_op jit(solution)/shard_map/all_to_all | solution.py:295
  168.4 7.0 %shard_map.126 = f32[4,512,256]{2,1,0:T(8,128)} custom-call(f32[1024,512]{1,0:T(8,128)S(1)} %bitcast.36, bf16[1024,1024]{1,0:T(8,128)(2,1)} %get-tuple-element.6.high_ref, bf16[1024,1024]{1,0:T(8,128)(2,1)} %get-tuple-element.7.low_ref), custom_call_target="tpu_custom_call" | custom-call | tf_op jit(solution)/shard_map/pallas_call | solution.py:134
  175.4 4.6 all-to-all-start.3
  188.1 17.1 %all-to-all-done.3 = f32[4,512,256]{2,1,0:T(8,128)} async-done(((f32[4,512,256]{2,1,0:T(8,128)}), f32[4,512,256]{2,1,0:T(8,128)}, u32[]{:S(2)}, u32[]{:S(2)}) %all-to-all-start.3) | async-done | bytes 2097184 | tf_op jit(solution)/shard_map/all_to_all | solution.py:298
  216.7 4.5 collective-permute-start.2
  237.1 5.0 %select_maximum_fusion.8 = f32[18,130,258]{2,1,0:T(8,128)} fusion(f32[16,130,1]{2,1,0:T(8,128)S(1)} %copy.48, f32[16,130,1]{2,1,0:T(8,128)} %copy.47, f32[16,1,256]{2,1,0:T(1,128)S(1)} %collective-permute-done.1, f32[16,128,256]{2,1,0:T(8,128)S(1)} %copy-done.8, f32[16,1,256]{2,1,0:T(1,128)S(1)} %collective-permute-done), kind=kLoop, calls=%fused_computation.10 | loop fusion | flops 7244640 | bytes 4561440 | tf_op jit(solution)/shard_map/concatenate | solution.py:25
  250.1 11.3 %multiply_multiply_fusion = (f32[16,128,256]{2,1,0:T(8,128)S(1)}, f32[16,128,256]{2,1,0:T(8,128)}) fusion(f32[256]{0:T(256)S(1)} %copy-done.20, f32[128]{0:T(128)S(1)} %copy-done.21, f32[16,128,256]{2,1,0:T(8,128)} %param.11, f32[4,16,32,256]{3,2,0,1:T(8,128)} %copy-done.16, s32[16,128,256]{2,1,0:T(8,128)S(1)} %copy-done.14, ...), kind=kLoop, calls=%fused_computation.93 | loop fusion | flops 31981568 | bytes 23169024 | tf_op jit(solution)/shard_map/mul | solution.py:285
  261.5 31.8 %all_to_all.41.in_ref = f32[4,512,256]{2,1,0:T(8,128)S(1)} all-to-all(f32[4,512,256]{2,1,0:T(8,128)S(1)} %bitcast.43), channel_id=1, replica_groups=mesh['gx'=4,'gy'=8] {'gx'}, dimensions={0} | all-to-all | bytes 4194304 | tf_op jit(solution)/shard_map/all_to_all | solution.py:288
  293.3 6.7 %shard_map.127 = f32[1024,512]{1,0:T(8,128)S(1)} custom-call(f32[4,512,256]{2,1,0:T(8,128)S(1)} %all_to_all.41.in_ref, bf16[1024,1024]{1,0:T(8,128)(2,1)} %get-tuple-element.6.high_ref, bf16[1024,1024]{1,0:T(8,128)(2,1)} %get-tuple-element.7.low_ref), custom_call_target="tpu_custom_call" | custom-call | tf_op jit(solution)/shard_map/pallas_call | solution.py:111
  300.0 50.7 %all_to_all.42.in_ref = f32[32,32,512]{2,1,0:T(8,128)S(1)} all-to-all(f32[32,32,512]{2,1,0:T(8,128)S(1)} %bitcast.37), channel_id=1, replica_groups=mesh['gx'=4,'gy'=8] {'gy','gx'}, dimensions={0} | all-to-all | bytes 4194304 | tf_op jit(solution)/shard_map/all_to_all | solution.py:291
  350.7 19.4 %shard_map.128 = f32[32,32,512]{2,1,0:T(8,128)S(1)} custom-call(f32[32,32,512]{2,1,0:T(8,128)S(1)} %all_to_all.42.in_ref, bf16[1024,1024]{1,0:T(8,128)(2,1)} %get-tuple-element.8.high_ref, bf16[1024,1024]{1,0:T(8,128)(2,1)} %get-tuple-element.9.low_ref, f32[1,1024]{1,0:T(1,128)S(1)} %bitcast.39, f32[32,1]{1,0:T(8,128)S(1)} %copy.43.values_y_ref, ...), custom_call_target="tpu_custom_call" | custom-call | tf_op jit(solution)/shard_map/pallas_call | solution.py:245
  370.1 52.0 %all_to_all.43 = f32[32,32,512]{2,1,0:T(8,128)S(1)} all-to-all(f32[32,32,512]{2,1,0:T(8,128)S(1)} %shard_map.128), channel_id=1, replica_groups=mesh['gx'=4,'gy'=8] {'gy','gx'}, dimensions={0} | all-to-all | bytes 4194304 | tf_op jit(solution)/shard_map/all_to_all | solution.py:295
  422.2 5.7 %shard_map.129 = f32[4,512,256]{2,1,0:T(8,128)S(1)} custom-call(f32[1024,512]{1,0:T(8,128)S(1)} %bitcast.35, bf16[1024,1024]{1,0:T(8,128)(2,1)} %get-tuple-element.6.high_ref, bf16[1024,1024]{1,0:T(8,128)(2,1)} %get-tuple-element.7.low_ref), custom_call_target="tpu_custom_call" | custom-call | tf_op jit(solution)/shard_map/pallas_call | solution.py:134
  427.9 28.3 %all_to_all.44 = f32[4,512,256]{2,1,0:T(8,128)S(1)} all-to-all(f32[4,512,256]{2,1,0:T(8,128)S(1)} %shard_map.129), channel_id=1, replica_groups=mesh['gx'=4,'gy'=8] {'gx'}, dimensions={0} | all-to-all | bytes 4194304 | tf_op jit(solution)/shard_map/all_to_all | solution.py:298
  472.3 4.5 collective-permute-start.10
  484.4 10.9 %fusion.5 = f32[16,128,256]{2,1,0:T(8,128)} fusion(f32[16,128,256]{2,1,0:T(8,128)} %get-tuple-element.13, f32[16,128,256]{2,1,0:T(8,128)S(1)} %copy-done.12, f32[16,130,1]{2,1,0:T(8,128)} %copy.62, f32[16,1,256]{2,1,0:T(1,128)S(1)} %collective-permute-done.9, f32[16,1,256]{2,1,0:T(1,128)S(1)} %collective-permute-done.8, f32[16,130,1]{2,1,0:T(8,128)} %copy.63, ...), kind=kLoop, calls=%fused_computation.23 | loop fusion | flops 30932992 | bytes 21070336 | tf_op jit(solution)/shard_map/sub | solution.py:305
  (98 shorter events, 71.8 us)
Async XLA Ops:
  0.6 46.5 %copy-start = (f32[1024]{0:T(1024)S(1)}, f32[1024]{0:T(1024)}, u32[]{:S(2)}) copy-start(f32[1024]{0:T(1024)} %param.19) | copy-start | bytes 12292
  4.0 30.0 %all-to-all-start = ((f32[4,512,256]{2,1,0:T(8,128)}), f32[4,512,256]{2,1,0:T(8,128)S(1)}, u32[]{:S(2)}, u32[]{:S(2)}) async-start(f32[4,512,256]{2,1,0:T(8,128)} %bitcast.42), calls=%async_computation | async-start | bytes 4194304 | tf_op jit(solution)/shard_map/all_to_all | solution.py:288
  42.1 53.7 %all-to-all-start.1 = ((f32[32,32,512]{2,1,0:T(8,128)}), f32[32,32,512]{2,1,0:T(8,128)S(1)}, u32[]{:S(2)}, u32[]{:S(2)}) async-start(f32[32,32,512]{2,1,0:T(8,128)} %bitcast.34), calls=%async_computation.1 | async-start | bytes 4194304 | tf_op jit(solution)/shard_map/all_to_all | solution.py:291
  47.3 48.5 %copy-start.3 = (f32[1024]{0:T(1024)S(1)}, f32[1024]{0:T(1024)}, u32[]{:S(2)}) copy-start(f32[1024]{0:T(1024)} %param.16) | copy-start | bytes 12292
  47.3 48.5 %copy-start.4 = (f32[16]{0:T(128)S(1)}, f32[16]{0:T(128)}, u32[]{:S(2)}) copy-start(f32[16]{0:T(128)} %diag_ref.3) | copy-start | bytes 196
  47.3 48.5 %copy-start.5 = (f32[15]{0:T(128)S(1)}, f32[15]{0:T(128)}, u32[]{:S(2)}) copy-start(f32[15]{0:T(128)} %coup_ref.3) | copy-start | bytes 184
  175.4 29.9 %all-to-all-start.3 = ((f32[4,512,256]{2,1,0:T(8,128)}), f32[4,512,256]{2,1,0:T(8,128)}, u32[]{:S(2)}, u32[]{:S(2)}) async-start(f32[4,512,256]{2,1,0:T(8,128)} %shard_map.126), calls=%async_computation.3 | async-start | bytes 4194304 | tf_op jit(solution)/shard_map/all_to_all | solution.py:298
  180.1 3.1 collective-permute-start
  181.8 4.7 collective-permute-start.1
  208.8 15.3 %collective-permute-start.4 = (f32[16,1,256]{2,1,0:T(1,128)S(1)}, f32[16,1,256]{2,1,0:T(1,128)S(1)}, u32[]{:S(2)}, u32[]{:S(2)}) collective-permute-start(f32[16,1,256]{2,1,0:T(1,128)S(1)} %get-tuple-element.26), channel_id=1, source_target_pairs={{0,1},{1,2},{2,3},{3,4},{4,5},{5,6},{6,7},{8,9},{9,10},{10,11},{11... | collective-permute-start | bytes 49160 | tf_op jit(solution)/shard_map/ppermute | solution.py:21
  210.3 13.9 %collective-permute-start.5 = (f32[16,1,256]{2,1,0:T(1,128)S(1)}, f32[16,1,256]{2,1,0:T(1,128)S(1)}, u32[]{:S(2)}, u32[]{:S(2)}) collective-permute-start(f32[16,1,256]{2,1,0:T(1,128)S(1)} %get-tuple-element.27), channel_id=1, source_target_pairs={{1,0},{2,1},{3,2},{4,3},{5,4},{6,5},{7,6},{9,8},{10,9},{11,10},{12... | collective-permute-start | bytes 49160 | tf_op jit(solution)/shard_map/ppermute | solution.py:24
  214.8 6.5 %collective-permute-start.3 = (f32[16,130,1]{1,0,2:T(8,128)S(1)}, f32[16,130,1]{1,0,2:T(8,128)S(1)}, u32[]{:S(2)}, u32[]{:S(2)}) collective-permute-start(f32[16,130,1]{1,0,2:T(8,128)S(1)} %copy.46), channel_id=1, source_target_pairs={{8,0},{16,8},{24,16},{9,1},{17,9},{25,17},{10,2},{18,10},{26,18},{... | collective-permute-start | bytes 24968 | tf_op jit(solution)/shard_map/ppermute | solution.py:24
  216.7 6.0 %collective-permute-start.2 = (f32[16,130,1]{1,0,2:T(8,128)S(1)}, f32[16,130,1]{1,0,2:T(8,128)S(1)}, u32[]{:S(2)}, u32[]{:S(2)}) collective-permute-start(f32[16,130,1]{1,0,2:T(8,128)S(1)} %copy.45), channel_id=1, source_target_pairs={{0,8},{8,16},{16,24},{1,9},{9,17},{17,25},{2,10},{10,18},{18,26},{... | collective-permute-start | bytes 24968 | tf_op jit(solution)/shard_map/ppermute | solution.py:21
  231.4 12.6 %collective-permute-start.6 = (f32[16,130,1]{1,0,2:T(8,128)S(1)}, f32[16,130,1]{1,0,2:T(8,128)S(1)}, u32[]{:S(2)}, u32[]{:S(2)}) collective-permute-start(f32[16,130,1]{1,0,2:T(8,128)S(1)} %copy.49), channel_id=1, source_target_pairs={{0,8},{8,16},{16,24},{1,9},{9,17},{17,25},{2,10},{10,18},{18,26},{... | collective-permute-start | bytes 24968 | tf_op jit(solution)/shard_map/ppermute | solution.py:21
  235.6 6.9 %collective-permute-start.7 = (f32[16,130,1]{1,0,2:T(8,128)S(1)}, f32[16,130,1]{1,0,2:T(8,128)S(1)}, u32[]{:S(2)}, u32[]{:S(2)}) collective-permute-start(f32[16,130,1]{1,0,2:T(8,128)S(1)} %copy.50), channel_id=1, source_target_pairs={{8,0},{16,8},{24,16},{9,1},{17,9},{25,17},{10,2},{18,10},{26,18},{... | collective-permute-start | bytes 24968 | tf_op jit(solution)/shard_map/ppermute | solution.py:24
  245.4 4.6 copy-start.14
  245.4 4.6 copy-start.20
  459.8 5.7 %copy-start.11 = (f32[16,128,256]{2,1,0:T(8,128)}, f32[16,128,256]{2,1,0:T(8,128)S(1)}, u32[]{:S(2)}) copy-start(f32[16,128,256]{2,1,0:T(8,128)S(1)} %get-tuple-element.22) | copy-start | bytes 6291460
  459.8 2.6 collective-permute-start.8
  461.1 4.1 collective-permute-start.9
  469.1 7.7 %collective-permute-start.11 = (f32[16,130,1]{1,0,2:T(8,128)S(1)}, f32[16,130,1]{1,0,2:T(8,128)S(1)}, u32[]{:S(2)}, u32[]{:S(2)}) collective-permute-start(f32[16,130,1]{1,0,2:T(8,128)S(1)} %copy.61), channel_id=1, source_target_pairs={{8,0},{16,8},{24,16},{9,1},{17,9},{25,17},{10,2},{18,10},{26,18},{... | collective-permute-start | bytes 24968 | tf_op jit(solution)/shard_map/ppermute | solution.py:24
  472.3 6.1 %collective-permute-start.10 = (f32[16,130,1]{1,0,2:T(8,128)S(1)}, f32[16,130,1]{1,0,2:T(8,128)S(1)}, u32[]{:S(2)}, u32[]{:S(2)}) collective-permute-start(f32[16,130,1]{1,0,2:T(8,128)S(1)} %copy.60), channel_id=1, source_target_pairs={{0,8},{8,16},{16,24},{1,9},{9,17},{17,25},{2,10},{10,18},{18,26},{... | collective-permute-start | bytes 24968 | tf_op jit(solution)/shard_map/ppermute | solution.py:21
  479.8 4.6 copy-start.15
  484.4 10.9 %copy-start.1 = (f32[1024]{0:T(1024)S(1)}, f32[1024]{0:T(1024)}, u32[]{:S(2)}) copy-start(f32[1024]{0:T(1024)} %param.19) | copy-start | bytes 12292
  (13 other events, 43.8 us)

commit v2 on v1

--- a/solution.py
+++ b/solution.py
@@ -13,49 +13,161 @@
 storage_term = 0.2
 
 
-def padded_2(block, sides, width):
-    for axis, dim in sides:
-        count = lax.axis_size(axis)
-        forward = [(i, i + 1) for i in range(count - 1)]
-        backward = [(target, source) for source, target in forward]
-        low = lax.ppermute(
-            lax.slice_in_dim(block, block.shape[dim] - width, None, axis=dim), axis, forward
-        )
-        high = lax.ppermute(lax.slice_in_dim(block, 0, width, axis=dim), axis, backward)
-        block = jnp.concatenate([low, block, high], axis=dim)
-    return block
-
-
 def harmonic(first, second):
     return 2.0 * first * second / (first + second)
 
 
-def neighbours(padded):
-    return [
-        padded[2:, 1:-1, 1:-1],
-        padded[:-2, 1:-1, 1:-1],
-        padded[1:-1, 2:, 1:-1],
-        padded[1:-1, :-2, 1:-1],
-        padded[1:-1, 1:-1, 2:],
-        padded[1:-1, 1:-1, :-2],
+def apply_kernel(
+    first, scale, back_ref, conduct_ref, active_ref, residual_ref, *refs
+):
+    refs = list(refs)
+    adjoint_ref = None if first else refs.pop(0)
+    mass_x_ref, mass_y_ref = (refs.pop(0), refs.pop(0)) if scale else (None, None)
+    new_adjoint_ref, new_residual_ref = refs.pop(0), refs.pop(0)
+    scaled_ref = refs.pop(0) if scale else None
+    masked, held, out_x, in_x, out_y, in_y, send_sem, recv_sem = refs
+    levels, rows, part_y = conduct_ref.shape
+    columns, part_x = back_ref.shape[0], back_ref.shape[2]
+    ix, iy = lax.axis_index("gx"), lax.axis_index("gy")
+    nx, ny = lax.axis_size("gx"), lax.axis_size("gy")
+    sides = [
+        (lax.rem(iy + 1, ny), ix, iy),
+        (lax.rem(iy + ny - 1, ny), ix, iy),
+        (iy, lax.rem(ix + 1, nx), ix),
+        (iy, lax.rem(ix + nx - 1, nx), ix),
     ]
-
-
-def faces_from(padded):
-    center = padded[1:-1, 1:-1, 1:-1]
-    return [harmonic(center, other) for other in neighbours(padded)]
-
-
-def stencil(padded, faces):
-    center = padded[1:-1, 1:-1, 1:-1]
-    result = storage_term * center
-    for face, other in zip(faces, neighbours(padded)):
-        result = result + face * (center - other)
-    return result
-
-
-def pad_vertical(values):
-    return jnp.pad(values, ((1, 1), (0, 0), (0, 0)))
+    barrier = pltpu.get_barrier_semaphore()
+    for line, column, _ in sides:
+        pl.semaphore_signal(
+            barrier, inc=1, device_id=(column, line), device_id_type=pl.DeviceIdType.MESH
+        )
+
+    out_y[...] = jnp.zeros_like(out_y)
+    for plane in (0, levels + 1):
+        masked[plane] = jnp.zeros((rows, part_y), jnp.float32)
+        held[plane] = jnp.zeros((rows, part_y), jnp.float32)
+
+    @pl.loop(0, levels)
+    def _(z):
+        update = jnp.concatenate([back_ref[s, z] for s in range(columns)], axis=0)
+        value = active_ref[z].astype(jnp.float32) * update
+        conduct = conduct_ref[z]
+        masked[z + 1] = value
+        held[z + 1] = conduct
+        for field, plane in enumerate((value, conduct)):
+            at = field * levels + z
+            out_x[0, pl.ds(at, 1), :] = plane[rows - 1 :, :]
+            out_x[1, pl.ds(at, 1), :] = plane[:1, :]
+            out_y[0, pl.ds(at, 1), :rows] = jnp.transpose(plane[:, part_y - LANES :])[LANES - 1 :, :]
+            out_y[1, pl.ds(at, 1), :rows] = jnp.transpose(plane[:, :LANES])[:1, :]
+
+    pl.semaphore_wait(barrier, 4)
+    copies = []
+    for k, (line, column, _) in enumerate(sides):
+        source, target = (out_x, in_x) if k < 2 else (out_y, in_y)
+        copies.append(
+            pltpu.make_async_remote_copy(
+                src_ref=source.at[k % 2],
+                dst_ref=target.at[k % 2],
+                send_sem=send_sem.at[k],
+                recv_sem=recv_sem.at[k],
+                device_id=(column, line),
+                device_id_type=pl.DeviceIdType.MESH,
+            )
+        )
+        copies[-1].start()
+    for copy in copies:
+        copy.wait()
+
+    inside = [
+        jnp.where(iy > 0, 1.0, 0.0),
+        jnp.where(iy < ny - 1, 1.0, 0.0),
+        jnp.where(ix > 0, 1.0, 0.0),
+        jnp.where(ix < nx - 1, 1.0, 0.0),
+    ]
+    row = lax.broadcasted_iota(jnp.int32, (rows, part_y), 0)
+    lane = lax.broadcasted_iota(jnp.int32, (rows, part_y), 1)
+
+    def upright(values):
+        tall = jnp.transpose(jnp.broadcast_to(values, (LANES, LANES)))[:rows]
+        return jnp.concatenate([tall] * (part_y // LANES), axis=1)
+
+    @pl.loop(0, levels)
+    def _(z):
+        center, conduct = masked[z + 1], held[z + 1]
+        result = storage_term * center
+
+        def add(result, other, other_conduct):
+            return result + harmonic(conduct, other_conduct) * (center - other)
+
+        result = add(result, masked[z + 2], held[z + 2])
+        result = add(result, masked[z], held[z])
+        at, at_conduct = pl.ds(z, 1), pl.ds(levels + z, 1)
+        result = add(
+            result,
+            jnp.where(row == rows - 1, in_x[1, at, :], pltpu.roll(center, rows - 1, 0)),
+            jnp.where(
+                row == rows - 1, in_x[1, at_conduct, :] * inside[1], pltpu.roll(conduct, rows - 1, 0)
+            ),
+        )
+        result = add(
+            result,
+            jnp.where(row == 0, in_x[0, at, :], pltpu.roll(center, 1, 0)),
+            jnp.where(row == 0, in_x[0, at_conduct, :] * inside[0], pltpu.roll(conduct, 1, 0)),
+        )
+        result = add(
+            result,
+            jnp.where(lane == part_y - 1, upright(in_y[1, at, :]), pltpu.roll(center, part_y - 1, 1)),
+            jnp.where(
+                lane == part_y - 1,
+                upright(in_y[1, at_conduct, :]) * inside[3],
+                pltpu.roll(conduct, part_y - 1, 1),
+            ),
+        )
+        result = add(
+            result,
+            jnp.where(lane == 0, upright(in_y[0, at, :]), pltpu.roll(center, 1, 1)),
+            jnp.where(
+                lane == 0, upright(in_y[0, at_conduct, :]) * inside[2], pltpu.roll(conduct, 1, 1)
+            ),
+        )
+        update = jnp.concatenate([back_ref[s, z] for s in range(columns)], axis=0)
+        active = active_ref[z].astype(jnp.float32)
+        residual = residual_ref[z] - (result + (1.0 - active) * update)
+        new_residual_ref[z] = residual
+        new_adjoint_ref[z] = update if first else adjoint_ref[z] + update
+        if scale:
+            scaled = residual * mass_x_ref[...] * mass_y_ref[...]
+            for s in range(columns):
+                scaled_ref[s, z] = scaled[s * part_x : (s + 1) * part_x, :]
+
+
+def apply_update(iteration, back, conduct, excavated, residual, adjoint, mass_x, mass_y):
+    first, scale = iteration == 0, iteration < ITERS - 1
+    levels, rows, part_y = conduct.shape
+    operands = [back, conduct, excavated, residual]
+    if not first:
+        operands.append(adjoint)
+    if scale:
+        operands += [mass_x[:, None], mass_y[None, :]]
+    field = jax.ShapeDtypeStruct(conduct.shape, jnp.float32)
+    outputs = [field, field]
+    if scale:
+        outputs.append(jax.ShapeDtypeStruct(back.shape, jnp.float32))
+    vmem = pl.BlockSpec(memory_space=VMEM)
+    return pl.pallas_call(
+        functools.partial(apply_kernel, first, scale),
+        out_shape=outputs,
+        in_specs=[vmem] * len(operands),
+        out_specs=[vmem] * len(outputs),
+        scratch_shapes=[VMEM((levels + 2, rows, part_y), jnp.float32)] * 2
+        + [VMEM((2, 2 * levels, part_y), jnp.float32)] * 2
+        + [VMEM((2, 2 * levels, LANES), jnp.float32)] * 2
+        + [pltpu.SemaphoreType.DMA((4,))] * 2,
+        compiler_params=pltpu.CompilerParams(
+            collective_id=iteration, has_side_effects=True, vmem_limit_bytes=48 << 20
+        ),
+    )(*operands)
 
 
 def split(value):
@@ -272,18 +384,15 @@
     part_x = rows // columns
     modes = vectors_y.shape[1] // devices
     both = ("gy", "gx")
-    active = excavated.astype(jnp.float32)
-    rim_conduct = padded_2(conduct, (("gy", 1), ("gx", 2)), 1)
-    faces = faces_from(pad_vertical(rim_conduct))
     high_x, low_x = split_matrix(vectors_x)
     high_y, low_y = split_matrix(vectors_y)
     start = (lax.axis_index("gy") * columns + lax.axis_index("gx")) * modes
     local_values = lax.dynamic_slice_in_dim(values_y, start, modes, 0)
-    adjoint = jnp.zeros_like(right_side)
+    adjoint = None
     residual = right_side
+    scaled = residual * mass_x[None, :, None] * mass_y[None, None, :]
+    scaled = scaled.reshape(levels, columns, part_x, part_y).transpose(1, 0, 2, 3)
     for iteration in range(ITERS):
-        scaled = residual * mass_x[None, :, None] * mass_y[None, None, :]
-        scaled = scaled.reshape(levels, columns, part_x, part_y).transpose(1, 0, 2, 3)
         scaled = scaled.reshape(columns, levels * part_x, part_y)
         got = lax.all_to_all(scaled, "gx", split_axis=0, concat_axis=0, tiled=True)
         lines_y = forward_y(got, high_y, low_y)
@@ -296,13 +405,11 @@
         got = got.reshape(devices * modes, levels * part_x)
         back = inverse_y(got, high_y, low_y, columns)
         back = lax.all_to_all(back, "gx", split_axis=0, concat_axis=0, tiled=True)
-        back = back.reshape(columns, levels, part_x, part_y).transpose(1, 0, 2, 3)
-        update = back.reshape(levels, rows, part_y)
-        adjoint = adjoint + update
-        masked = active * update
-        rim_masked = padded_2(masked, (("gy", 1), ("gx", 2)), 1)
-        image = stencil(pad_vertical(rim_masked), faces) + (1.0 - active) * update
-        residual = residual - image
+        back = back.reshape(columns, levels, part_x, part_y)
+        adjoint, residual, *rest = apply_update(
+            iteration, back, conduct, excavated, residual, adjoint, mass_x, mass_y
+        )
+        scaled = rest[0] if rest else None
     return (adjoint, residual)
 
 

time: 498 us -> 441 us (0.89)
  other arithmetic: 44 us -> 1.9 us
  Pallas kernels: 78.4 us -> 114 us
  starting transfers between devices: 40.5 us -> 14.8 us
  local copies, waits for them, and re-layouts: 30.8 us -> 8.4 us
    pallas_call x0 -> x2, Pallas kernels: none -> 35.1 us  [apply_update(): pl.pallas_call(functools.partial(apply_kernel, first, scale), out_shape=o...]
    ppermute x12 -> x0, starting transfers between devices: 25.8 us -> none  [the longest x6 17.8 us: padded_2(): lax.ppermute(lax.slice_in_dim(block, block.shape[dim] - width, None, axis...]
    concatenate x6 -> x0, other arithmetic: 17.5 us -> none  [padded_2(): block = jnp.concatenate([low, block, high], axis=dim)]
    slice x12 -> x0, local copies, waits for them, and re-layouts: 14.8 us -> none  [the longest x6 10.4 us: padded_2(): lax.slice_in_dim(block, 0, width, axis=dim)]
    mul x2 -> x1, other arithmetic: 13.2 us -> 1.9 us  [shards(): scaled = residual * mass_x[None, :, None] * mass_y[None, None, :]]
    sub x1 -> x0, other arithmetic: 10.9 us -> none  [shards(): residual = residual - image]
    all_to_all x1, waiting for transfers between devices: 17.1 us -> 25.2 us  [shards(): back = lax.all_to_all(back, 'gx', split_axis=0, concat_axis=0, tiled=True)]
    ppermute x6 -> x0, local copies, waits for them, and re-layouts: 7.73 us -> none  [the longest x3 4.33 us: padded_2(): lax.ppermute(lax.slice_in_dim(block, block.shape[dim] - width, None, axis...]
  transfers between devices with their start and end apart: 15 -> 3, of which waited for: 7 -> 3; matrix products, arithmetic and copies ran while one was open for 4% -> 0% of each run, Pallas kernels for 3% -> 3%
where the time goes in v2:
time: 441 us; the launch traced here: 440 us
  blocking collectives  215 us (49%)
  Pallas kernels  114 us (26%)
  waiting for transfers between devices  85.1 us (19%)
  starting transfers between devices  14.8 us (3%)
  local copies, waits for them, and re-layouts  8.4 us (2%)
    all_to_all x2, blocking collectives, shards(): got = lax.all_to_all(solved, both, split_axis=0, concat_axis=0, tiled=True)  105 us
    all_to_all x1, blocking collectives, shards(): got = lax.all_to_all(lines_y, both, split_axis=0, concat_axis=0, tiled=True)  51.7 us
    all_to_all x1, waiting for transfers between devices, shards(): got = lax.all_to_all(lines_y, both, split_axis=0, concat_axis=0, tiled=True)  41.8 us
    pallas_call x2, Pallas kernels, middle(): pl.pallas_call(middle_kernel, out_shape=jax.ShapeDtypeStruct(values.shape...  38.8 us
    pallas_call x2, Pallas kernels, apply_update(): pl.pallas_call(functools.partial(apply_kernel, first, scale), out_shape=o...  35.1 us
    all_to_all x1, blocking collectives, shards(): got = lax.all_to_all(scaled, 'gx', split_axis=0, concat_axis=0, tiled=True)  29.4 us
    all_to_all x1, blocking collectives, shards(): back = lax.all_to_all(back, 'gx', split_axis=0, concat_axis=0, tiled=True)  28.9 us
    all_to_all x1, waiting for transfers between devices, shards(): back = lax.all_to_all(back, 'gx', split_axis=0, concat_axis=0, tiled=True)  25.2 us
  transfers between devices with their start and end apart: 3, of which 3 were waited for; matrix products, arithmetic and copies ran while one was open for 0% of the time, Pallas kernels for 3%

profile of v2, /device:TPU:0, one launch (start us, length us, event | category | flops | bytes accessed | tf_op | source)
XLA Modules:
  0.0 439.8 jit_solution(3214736708781591043)
XLA Ops:
  0.6 1.9 multiply_multiply_fusion
  2.6 1.5 copy.13
  4.0 5.2 %all-to-all-start = ((f32[4,512,256]{2,1,0:T(8,128)}), f32[4,512,256]{2,1,0:T(8,128)S(1)}, u32[]{:S(2)}, u32[]{:S(2)}) async-start(f32[4,512,256]{2,1,0:T(8,128)} %bitcast.25), calls=%async_computation | async-start | bytes 4194304 | tf_op jit(solution)/shard_map/all_to_all | solution.py:397
  9.2 6.7 %shard_map.122 = (bf16[1024,1024]{1,0:T(8,128)(2,1)}, bf16[1024,1024]{1,0:T(8,128)(2,1)}) custom-call(f32[1024,1024]{1,0:T(8,128)} %in_ref.2), custom_call_target="tpu_custom_call" | custom-call | tf_op jit(solution)/shard_map/pallas_call | solution.py:192
  15.9 18.2 %all-to-all-done.in_ref = f32[4,512,256]{2,1,0:T(8,128)S(1)} async-done(((f32[4,512,256]{2,1,0:T(8,128)}), f32[4,512,256]{2,1,0:T(8,128)S(1)}, u32[]{:S(2)}, u32[]{:S(2)}) %all-to-all-start) | async-done | bytes 2097184 | tf_op jit(solution)/shard_map/all_to_all | solution.py:397
  34.0 6.7 %shard_map.123 = f32[1024,512]{1,0:T(8,128)S(1)} custom-call(f32[4,512,256]{2,1,0:T(8,128)S(1)} %all-to-all-done.in_ref, bf16[1024,1024]{1,0:T(8,128)(2,1)} %get-tuple-element.9.high_ref, bf16[1024,1024]{1,0:T(8,128)(2,1)} %get-tuple-element.10.low_ref), custom_call_target="tpu_custom_call" | custom-call | tf_op jit(solution)/shard_map/pallas_call | solution.py:223
  42.1 5.0 %all-to-all-start.1 = ((f32[32,32,512]{2,1,0:T(8,128)}), f32[32,32,512]{2,1,0:T(8,128)S(1)}, u32[]{:S(2)}, u32[]{:S(2)}) async-start(f32[32,32,512]{2,1,0:T(8,128)} %bitcast.16), calls=%async_computation.1 | async-start | bytes 4194304 | tf_op jit(solution)/shard_map/all_to_all | solution.py:400
  47.3 6.7 %shard_map.124 = (bf16[1024,1024]{1,0:T(8,128)(2,1)}, bf16[1024,1024]{1,0:T(8,128)(2,1)}) custom-call(f32[1024,1024]{1,0:T(8,128)} %in_ref.3), custom_call_target="tpu_custom_call" | custom-call | tf_op jit(solution)/shard_map/pallas_call | solution.py:192
  54.1 41.8 %all-to-all-done.1.in_ref = f32[32,32,512]{2,1,0:T(8,128)S(1)} async-done(((f32[32,32,512]{2,1,0:T(8,128)}), f32[32,32,512]{2,1,0:T(8,128)S(1)}, u32[]{:S(2)}, u32[]{:S(2)}) %all-to-all-start.1) | async-done | bytes 2097184 | tf_op jit(solution)/shard_map/all_to_all | solution.py:400
  95.9 19.4 %shard_map.125 = f32[32,32,512]{2,1,0:T(8,128)S(1)} custom-call(f32[32,32,512]{2,1,0:T(8,128)S(1)} %all-to-all-done.1.in_ref, bf16[1024,1024]{1,0:T(8,128)(2,1)} %get-tuple-element.11.high_ref, bf16[1024,1024]{1,0:T(8,128)(2,1)} %get-tuple-element.12.low_ref, f32[1,1024]{1,0:T(1,128)S(1)} %bitcast.20, f32[32,1]{1,0:T(8,128)S(1)} %copy.14.values_y_ref, ...), custom_call_target="tpu_custom_call" | custom-call | tf_op jit(solution)/shard_map/pallas_call | solution.py:357
  115.3 53.1 %all_to_all.40 = f32[32,32,512]{2,1,0:T(8,128)S(1)} all-to-all(f32[32,32,512]{2,1,0:T(8,128)S(1)} %shard_map.125), channel_id=1, replica_groups=mesh['gx'=4,'gy'=8] {'gy','gx'}, dimensions={0} | all-to-all | bytes 4194304 | tf_op jit(solution)/shard_map/all_to_all | solution.py:404
  168.4 7.0 %shard_map.126 = f32[4,512,256]{2,1,0:T(8,128)} custom-call(f32[1024,512]{1,0:T(8,128)S(1)} %bitcast.18, bf16[1024,1024]{1,0:T(8,128)(2,1)} %get-tuple-element.9.high_ref, bf16[1024,1024]{1,0:T(8,128)(2,1)} %get-tuple-element.10.low_ref), custom_call_target="tpu_custom_call" | custom-call | tf_op jit(solution)/shard_map/pallas_call | solution.py:246
  175.4 4.6 %all-to-all-start.3 = ((f32[4,512,256]{2,1,0:T(8,128)}), f32[4,512,256]{2,1,0:T(8,128)}, u32[]{:S(2)}, u32[]{:S(2)}) async-start(f32[4,512,256]{2,1,0:T(8,128)} %shard_map.126), calls=%async_computation.3 | async-start | bytes 4194304 | tf_op jit(solution)/shard_map/all_to_all | solution.py:407
  180.1 25.2 %all-to-all-done.3 = f32[4,512,256]{2,1,0:T(8,128)} async-done(((f32[4,512,256]{2,1,0:T(8,128)}), f32[4,512,256]{2,1,0:T(8,128)}, u32[]{:S(2)}, u32[]{:S(2)}) %all-to-all-start.3) | async-done | bytes 2097184 | tf_op jit(solution)/shard_map/all_to_all | solution.py:407
  205.3 18.2 %shard_map.127 = (f32[16,128,256]{2,1,0:T(8,128)S(1)}, f32[16,128,256]{2,1,0:T(8,128)S(1)}, f32[4,16,32,256]{3,2,1,0:T(8,128)}) custom-call(f32[4,16,32,256]{3,2,1,0:T(8,128)} %bitcast.7.back_ref, f32[16,128,256]{2,1,0:T(8,128)} %conduct_ref.3, s32[16,128,256]{2,1,0:T(8,128)} %active_ref.3, f32[16,128,256]{2,1,0:T(8,128)} %residual_ref.1, ...), custom_call_target="tpu_custom_call" | custom-call | tf_op jit(solution)/shard_map/pallas_call | solution.py:158
  223.6 1.3 copy-done.3
  226.2 29.4 %all_to_all.41.in_ref = f32[4,512,256]{2,1,0:T(8,128)S(1)} all-to-all(f32[4,512,256]{2,1,0:T(8,128)} %bitcast.26), channel_id=1, replica_groups=mesh['gx'=4,'gy'=8] {'gx'}, dimensions={0} | all-to-all | bytes 4194304 | tf_op jit(solution)/shard_map/all_to_all | solution.py:397
  255.6 6.7 %shard_map.128 = f32[1024,512]{1,0:T(8,128)S(1)} custom-call(f32[4,512,256]{2,1,0:T(8,128)S(1)} %all_to_all.41.in_ref, bf16[1024,1024]{1,0:T(8,128)(2,1)} %get-tuple-element.9.high_ref, bf16[1024,1024]{1,0:T(8,128)(2,1)} %get-tuple-element.10.low_ref), custom_call_target="tpu_custom_call" | custom-call | tf_op jit(solution)/shard_map/pallas_call | solution.py:223
  262.3 51.7 %all_to_all.42.in_ref = f32[32,32,512]{2,1,0:T(8,128)S(1)} all-to-all(f32[32,32,512]{2,1,0:T(8,128)S(1)} %bitcast.19), channel_id=1, replica_groups=mesh['gx'=4,'gy'=8] {'gy','gx'}, dimensions={0} | all-to-all | bytes 4194304 | tf_op jit(solution)/shard_map/all_to_all | solution.py:400
  314.1 19.4 %shard_map.129 = f32[32,32,512]{2,1,0:T(8,128)S(1)} custom-call(f32[32,32,512]{2,1,0:T(8,128)S(1)} %all_to_all.42.in_ref, bf16[1024,1024]{1,0:T(8,128)(2,1)} %get-tuple-element.11.high_ref, bf16[1024,1024]{1,0:T(8,128)(2,1)} %get-tuple-element.12.low_ref, f32[1,1024]{1,0:T(1,128)S(1)} %bitcast.21, f32[32,1]{1,0:T(8,128)S(1)} %copy.14.values_y_ref, ...), custom_call_target="tpu_custom_call" | custom-call | tf_op jit(solution)/shard_map/pallas_call | solution.py:357
  333.5 52.1 %all_to_all.43 = f32[32,32,512]{2,1,0:T(8,128)S(1)} all-to-all(f32[32,32,512]{2,1,0:T(8,128)S(1)} %shard_map.129), channel_id=1, replica_groups=mesh['gx'=4,'gy'=8] {'gy','gx'}, dimensions={0} | all-to-all | bytes 4194304 | tf_op jit(solution)/shard_map/all_to_all | solution.py:404
  385.6 5.7 %shard_map.130 = f32[4,512,256]{2,1,0:T(8,128)S(1)} custom-call(f32[1024,512]{1,0:T(8,128)S(1)} %bitcast.17, bf16[1024,1024]{1,0:T(8,128)(2,1)} %get-tuple-element.9.high_ref, bf16[1024,1024]{1,0:T(8,128)(2,1)} %get-tuple-element.10.low_ref), custom_call_target="tpu_custom_call" | custom-call | tf_op jit(solution)/shard_map/pallas_call | solution.py:246
  391.3 28.9 %all_to_all.44 = f32[4,512,256]{2,1,0:T(8,128)} all-to-all(f32[4,512,256]{2,1,0:T(8,128)S(1)} %shard_map.130), channel_id=1, replica_groups=mesh['gx'=4,'gy'=8] {'gx'}, dimensions={0} | all-to-all | bytes 4194304 | tf_op jit(solution)/shard_map/all_to_all | solution.py:407
  420.2 16.9 %shard_map.131 = (f32[16,128,256]{2,1,0:T(8,128)S(1)}, f32[16,128,256]{2,1,0:T(8,128)S(1)}) custom-call(f32[4,16,32,256]{3,2,1,0:T(8,128)} %bitcast.23, f32[16,128,256]{2,1,0:T(8,128)} %conduct_ref.3, s32[16,128,256]{2,1,0:T(8,128)} %active_ref.3, f32[16,128,256]{2,1,0:T(8,128)} %copy-done.4, f32[16,128,256]{2,1,0:T(8,128)} %copy-done.3), custom_call_target="tpu_custom_call" | custom-call | tf_op jit(solution)/shard_map/pallas_call | solution.py:158
  (24 shorter events, 5.6 us)
Async XLA Ops:
  0.6 46.5 %copy-start = (f32[1024]{0:T(1024)S(1)}, f32[1024]{0:T(1024)}, u32[]{:S(2)}) copy-start(f32[1024]{0:T(1024)} %param.19) | copy-start | bytes 12292
  4.0 30.0 %all-to-all-start = ((f32[4,512,256]{2,1,0:T(8,128)}), f32[4,512,256]{2,1,0:T(8,128)S(1)}, u32[]{:S(2)}, u32[]{:S(2)}) async-start(f32[4,512,256]{2,1,0:T(8,128)} %bitcast.25), calls=%async_computation | async-start | bytes 4194304 | tf_op jit(solution)/shard_map/all_to_all | solution.py:397
  40.8 1.3 copy-start.2
  42.1 53.7 %all-to-all-start.1 = ((f32[32,32,512]{2,1,0:T(8,128)}), f32[32,32,512]{2,1,0:T(8,128)S(1)}, u32[]{:S(2)}, u32[]{:S(2)}) async-start(f32[32,32,512]{2,1,0:T(8,128)} %bitcast.16), calls=%async_computation.1 | async-start | bytes 4194304 | tf_op jit(solution)/shard_map/all_to_all | solution.py:400
  47.3 48.5 %copy-start.5 = (f32[1024]{0:T(1024)S(1)}, f32[1024]{0:T(1024)}, u32[]{:S(2)}) copy-start(f32[1024]{0:T(1024)} %param.16) | copy-start | bytes 12292
  47.3 48.5 %copy-start.7 = (f32[16]{0:T(128)S(1)}, f32[16]{0:T(128)}, u32[]{:S(2)}) copy-start(f32[16]{0:T(128)} %diag_ref.3) | copy-start | bytes 196
  47.3 48.5 %copy-start.8 = (f32[15]{0:T(128)S(1)}, f32[15]{0:T(128)}, u32[]{:S(2)}) copy-start(f32[15]{0:T(128)} %coup_ref.3) | copy-start | bytes 184
  175.4 4.6 %copy-start.9 = (f32[128]{0:T(128)S(1)}, f32[128]{0:T(128)}, u32[]{:S(2)}) copy-start(f32[128]{0:T(128)} %param.15) | copy-start | bytes 1540
  175.4 29.9 %copy-start.6 = (f32[256]{0:T(256)S(1)}, f32[256]{0:T(256)}, u32[]{:S(2)}) copy-start(f32[256]{0:T(256)} %param.18) | copy-start | bytes 3076
  175.4 29.9 %all-to-all-start.3 = ((f32[4,512,256]{2,1,0:T(8,128)}), f32[4,512,256]{2,1,0:T(8,128)}, u32[]{:S(2)}, u32[]{:S(2)}) async-start(f32[4,512,256]{2,1,0:T(8,128)} %shard_map.126), calls=%async_computation.3 | async-start | bytes 4194304 | tf_op jit(solution)/shard_map/all_to_all | solution.py:407
  223.5 1.4 copy-start.3
  224.9 1.3 copy-start.4
  437.1 2.7 copy-start.1

commit v3 on v2

--- a/solution.py
+++ b/solution.py
@@ -198,58 +198,167 @@
     )(matrix)
 
 
-def forward_y_kernel(in_ref, high_ref, low_ref, out_ref, low_in, high_in):
+MESH = pl.DeviceIdType.MESH
+
+
+def place():
+    columns, lines = lax.axis_size("gx"), lax.axis_size("gy")
+    ix, iy = lax.axis_index("gx"), lax.axis_index("gy")
+    return columns, columns * lines, ix, iy, iy * columns + ix
+
+
+def greet_all():
+    columns, devices, _, _, me = place()
+    barrier = pltpu.get_barrier_semaphore()
+
+    @pl.loop(1, devices)
+    def _(k):
+        to = lax.rem(me + k, devices)
+        pl.semaphore_signal(
+            barrier, inc=1, device_id=(lax.rem(to, columns), to // columns), device_id_type=MESH
+        )
+
+    pl.semaphore_wait(barrier, devices - 1)
+
+
+def send_to_all(source_ref, target_ref, lanes, send_sem, recv_sem):
+    columns, devices, _, _, me = place()
+
+    @pl.loop(1, devices)
+    def _(k):
+        to = lax.rem(me + k, devices)
+        pltpu.make_async_remote_copy(
+            src_ref=source_ref.at[to, :, lanes],
+            dst_ref=target_ref.at[me, :, lanes],
+            send_sem=send_sem,
+            recv_sem=recv_sem,
+            device_id=(lax.rem(to, columns), to // columns),
+            device_id_type=MESH,
+        ).start()
+
+
+def wait_for_all(ref, lanes, sem):
+    part = ref.at[pl.ds(0, ref.shape[0] - 1), :, lanes]
+    pltpu.make_async_copy(part, part, sem).wait()
+
+
+def row_copies(source_ref, target_ref, rows, send_sem, recv_sem):
+    columns, _, ix, iy, _ = place()
+    copies = []
+    for k in range(1, columns):
+        to = lax.rem(ix + k, columns)
+        copies.append(
+            pltpu.make_async_remote_copy(
+                src_ref=source_ref.at[to, rows],
+                dst_ref=target_ref.at[ix, rows],
+                send_sem=send_sem.at[k - 1],
+                recv_sem=recv_sem.at[k - 1],
+                device_id=(to, iy),
+                device_id_type=MESH,
+            )
+        )
+    return copies
+
+
+def forward_kernel(
+    in_ref, high_ref, low_ref, out_ref, got, lines, high_in, low_in, send_x, recv_x, send_all, recv_all
+):
     sources, count, part = in_ref.shape
-    for source in range(sources):
-        high, low = split(in_ref[source])
-        high_in[:, source * part : (source + 1) * part] = high
-        low_in[:, source * part : (source + 1) * part] = low
-    modes = high_ref.shape[1]
+    devices, modes, _ = out_ref.shape
+    _, _, ix, _, me = place()
+    chunks = count // LANES
     width = 256
-
-    @pl.loop(0, modes // width)
-    def _(step):
-        columns = pl.ds(pl.multiple_of(step * width, width), width)
-        out_ref[columns, :] = dot3(
-            (high_ref[:, columns], low_ref[:, columns]),
-            (high_in[...], low_in[...]),
-            ((0,), (1,)),
-        )
-
-
-def forward_y(values, high, low):
-    sources, count, part = values.shape
-    size = sources * part
+    greet_all()
+    copies = []
+    for chunk in range(chunks):
+        rows = slice(chunk * LANES, (chunk + 1) * LANES)
+        copies.append(row_copies(in_ref, got, rows, send_x.at[chunk], recv_x.at[chunk]))
+        for copy in copies[-1]:
+            copy.start()
+    got[ix] = in_ref[ix]
+    for chunk in range(chunks):
+        rows = slice(chunk * LANES, (chunk + 1) * LANES)
+        for copy in copies[chunk]:
+            copy.wait_recv()
+        for source in range(sources):
+            along = slice(source * part, (source + 1) * part)
+            high_in[:, along], low_in[:, along] = split(got[source, rows, :])
+
+        @pl.loop(0, devices * modes // width)
+        def _(step):
+            columns = pl.ds(pl.multiple_of(step * width, width), width)
+            made = dot3(
+                (high_ref[:, columns], low_ref[:, columns]),
+                (high_in[...], low_in[...]),
+                ((0,), (1,)),
+            )
+            blocks = width // modes
+            lines[pl.ds(step * blocks, blocks), :, rows] = made.reshape(blocks, modes, LANES)
+
+        send_to_all(lines, out_ref, rows, send_all.at[chunk], recv_all.at[chunk])
+        out_ref[me, :, rows] = lines[me, :, rows]
+    for chunk in range(chunks):
+        rows = slice(chunk * LANES, (chunk + 1) * LANES)
+        for copy in copies[chunk]:
+            copy.wait_send()
+        wait_for_all(lines, rows, send_all.at[chunk])
+        wait_for_all(out_ref, rows, recv_all.at[chunk])
+
+
+def inverse_kernel(
+    in_ref, high_ref, low_ref, out_ref, got, made, high_in, low_in, send_x, recv_x, send_all, recv_all
+):
+    targets, count, part = out_ref.shape
+    devices, modes, _ = in_ref.shape
+    _, _, ix, _, me = place()
+    chunks = count // LANES
+    greet_all()
+    for chunk in range(chunks):
+        rows = slice(chunk * LANES, (chunk + 1) * LANES)
+        send_to_all(in_ref, got, rows, send_all.at[chunk], recv_all.at[chunk])
+    got[me] = in_ref[me]
+    copies = []
+    for chunk in range(chunks):
+        rows = slice(chunk * LANES, (chunk + 1) * LANES)
+        wait_for_all(got, rows, recv_all.at[chunk])
+        moved = jnp.transpose(got[:, :, rows].reshape(devices * modes, LANES))
+        high_in[...], low_in[...] = split(moved)
+
+        @pl.loop(0, targets)
+        def _(target):
+            along = pl.ds(pl.multiple_of(target * part, part), part)
+            made[target, rows, :] = dot3(
+                (high_in[...], low_in[...]), (high_ref[along, :], low_ref[along, :]), ((1,), (1,))
+            )
+
+        copies.append(row_copies(made, out_ref, rows, send_x.at[chunk], recv_x.at[chunk]))
+        for copy in copies[-1]:
+            copy.start()
+        out_ref[ix, rows, :] = made[ix, rows, :]
+    for chunk in range(chunks):
+        rows = slice(chunk * LANES, (chunk + 1) * LANES)
+        for copy in copies[chunk]:
+            copy.wait()
+        wait_for_all(in_ref, rows, send_all.at[chunk])
+
+
+def y_transform(kernel, collective_id, values, high, low, rows_shape, lines_shape, forward):
+    count, size = rows_shape[1], high.shape[0]
+    chunks = count // LANES
+    rows_vmem, lines_vmem = VMEM(rows_shape, jnp.float32), VMEM(lines_shape, jnp.float32)
+    row_sems = pltpu.SemaphoreType.DMA((chunks, rows_shape[0] - 1))
     return pl.pallas_call(
-        forward_y_kernel,
-        out_shape=jax.ShapeDtypeStruct((size, count), jnp.float32),
+        kernel,
+        out_shape=jax.ShapeDtypeStruct(lines_shape if forward else rows_shape, jnp.float32),
         in_specs=[pl.BlockSpec(memory_space=VMEM)] * 3,
         out_specs=pl.BlockSpec(memory_space=VMEM),
-        scratch_shapes=[VMEM((count, size), jnp.bfloat16)] * 2,
-        compiler_params=pltpu.CompilerParams(vmem_limit_bytes=48 << 20),
-    )(values, high, low)
-
-
-def inverse_y_kernel(in_ref, high_ref, low_ref, out_ref, high_in, low_in):
-    targets, count, part = out_ref.shape
-    moved = jnp.transpose(in_ref[...])
-    high_in[...], low_in[...] = split(moved)
-    for target in range(targets):
-        rows = slice(target * part, (target + 1) * part)
-        out_ref[target] = dot3(
-            (high_in[...], low_in[...]), (high_ref[rows, :], low_ref[rows, :]), ((1,), (1,))
-        )
-
-
-def inverse_y(values, high, low, targets):
-    size, count = values.shape
-    return pl.pallas_call(
-        inverse_y_kernel,
-        out_shape=jax.ShapeDtypeStruct((targets, count, size // targets), jnp.float32),
-        in_specs=[pl.BlockSpec(memory_space=VMEM)] * 3,
-        out_specs=pl.BlockSpec(memory_space=VMEM),
-        scratch_shapes=[VMEM((count, size), jnp.bfloat16)] * 2,
-        compiler_params=pltpu.CompilerParams(vmem_limit_bytes=48 << 20),
+        scratch_shapes=([rows_vmem, lines_vmem] if forward else [lines_vmem, rows_vmem])
+        + [VMEM((LANES, size), jnp.bfloat16)] * 2
+        + [row_sems] * 2
+        + [pltpu.SemaphoreType.DMA((chunks,))] * 2,
+        compiler_params=pltpu.CompilerParams(
+            collective_id=collective_id, has_side_effects=True, vmem_limit_bytes=48 << 20
+        ),
     )(values, high, low)
 
 
@@ -383,7 +492,6 @@
     levels, rows, part_y = right_side.shape
     part_x = rows // columns
     modes = vectors_y.shape[1] // devices
-    both = ("gy", "gx")
     high_x, low_x = split_matrix(vectors_x)
     high_y, low_y = split_matrix(vectors_y)
     start = (lax.axis_index("gy") * columns + lax.axis_index("gx")) * modes
@@ -394,17 +502,16 @@
     scaled = scaled.reshape(levels, columns, part_x, part_y).transpose(1, 0, 2, 3)
     for iteration in range(ITERS):
         scaled = scaled.reshape(columns, levels * part_x, part_y)
-        got = lax.all_to_all(scaled, "gx", split_axis=0, concat_axis=0, tiled=True)
-        lines_y = forward_y(got, high_y, low_y)
-        lines_y = lines_y.reshape(devices, modes, levels * part_x)
-        got = lax.all_to_all(lines_y, both, split_axis=0, concat_axis=0, tiled=True)
+        lines_shape = (devices, modes, levels * part_x)
+        got = y_transform(
+            forward_kernel, ITERS, scaled, high_y, low_y, scaled.shape, lines_shape, True
+        )
         solved = middle(
             got, high_x, low_x, values_x, local_values, vertical_diag, vertical_coupling
         )
-        got = lax.all_to_all(solved, both, split_axis=0, concat_axis=0, tiled=True)
-        got = got.reshape(devices * modes, levels * part_x)
-        back = inverse_y(got, high_y, low_y, columns)
-        back = lax.all_to_all(back, "gx", split_axis=0, concat_axis=0, tiled=True)
+        back = y_transform(
+            inverse_kernel, ITERS + 1, solved, high_y, low_y, scaled.shape, lines_shape, False
+        )
         back = back.reshape(columns, levels, part_x, part_y)
         adjoint, residual, *rest = apply_update(
             iteration, back, conduct, excavated, residual, adjoint, mass_x, mass_y

time: 441 us -> 358 us (0.81)
  Pallas kernels: 114 us -> 343 us
  blocking collectives: 215 us -> 0 us
  waiting for transfers between devices: 85.1 us -> 0 us
  starting transfers between devices: 14.8 us -> 0 us
    pallas_call x4, Pallas kernels: 26.2 us -> 250 us  [y_transform(): pl.pallas_call(kernel, out_shape=jax.ShapeDtypeStruct(lines_shape if forw...]
    all_to_all x5 -> x0, blocking collectives: 215 us -> none  [the longest x2 105 us: shards(): got = lax.all_to_all(solved, both, split_axis=0, concat_axis=0, tiled=True)]
    all_to_all x3 -> x0, waiting for transfers between devices: 85.1 us -> none  [the longest x1 41.8 us: shards(): got = lax.all_to_all(lines_y, both, split_axis=0, concat_axis=0, tiled=True)]
    all_to_all x3 -> x0, starting transfers between devices: 14.8 us -> none  [the longest x1 5.16 us: shards(): got = lax.all_to_all(scaled, 'gx', split_axis=0, concat_axis=0, tiled=True)]
    pallas_call x2, Pallas kernels: 35.1 us -> 40.7 us  [apply_update(): pl.pallas_call(functools.partial(apply_kernel, first, scale), out_shape=o...]
  transfers between devices with their start and end apart: 3 -> 0, of which waited for: 3 -> 0; matrix products, arithmetic and copies ran while one was open for 0% -> 0% of each run, Pallas kernels for 3% -> 0%
where the time goes in v3:
time: 358 us; the launch traced here: 357 us
  Pallas kernels  343 us (96%)
  local copies, waits for them, and re-layouts  11.4 us (3%)
    pallas_call x4, Pallas kernels, y_transform(): pl.pallas_call(kernel, out_shape=jax.ShapeDtypeStruct(lines_shape if forw...  250 us
    pallas_call x2, Pallas kernels, apply_update(): pl.pallas_call(functools.partial(apply_kernel, first, scale), out_shape=o...  40.7 us
    pallas_call x2, Pallas kernels, middle(): pl.pallas_call(middle_kernel, out_shape=jax.ShapeDtypeStruct(values.shape...  38.9 us
    pallas_call x2, Pallas kernels, split_matrix(): pl.pallas_call(split_kernel, grid=(8,), out_shape=[jax.ShapeDtypeStruct(m...  13.3 us
    unnamed x22, local copies, waits for them, and re-layouts  10.2 us

profile of v3, /device:TPU:0, one launch (start us, length us, event | category | flops | bytes accessed | tf_op | source)
XLA Modules:
  0.0 357.3 jit_solution(14340062802151220573)
XLA Ops:
  0.6 0.0 copy-start
  0.7 0.7 copy-done
  1.3 0.1 dynamic-slice_bitcast_fusion
  1.4 0.1 copy.14.values_y_ref
  1.5 0.8 copy.15.refs_0_
  2.2 1.9 multiply_multiply_fusion
  4.2 0.2 copy.13
  4.4 6.7 %shard_map.124 = (bf16[1024,1024]{1,0:T(8,128)(2,1)}, bf16[1024,1024]{1,0:T(8,128)(2,1)}) custom-call(f32[1024,1024]{1,0:T(8,128)} %in_ref.3), custom_call_target="tpu_custom_call" | custom-call | tf_op jit(solution)/shard_map/pallas_call | solution.py:192
  11.1 6.6 %shard_map.122 = (bf16[1024,1024]{1,0:T(8,128)(2,1)}, bf16[1024,1024]{1,0:T(8,128)(2,1)}) custom-call(f32[1024,1024]{1,0:T(8,128)} %in_ref.2), custom_call_target="tpu_custom_call" | custom-call | tf_op jit(solution)/shard_map/pallas_call | solution.py:192
  17.7 62.2 %shard_map.123.in_ref = f32[32,32,512]{2,1,0:T(8,128)S(1)} custom-call(f32[4,512,256]{2,1,0:T(8,128)S(1)} %bitcast.14, bf16[1024,1024]{1,0:T(8,128)(2,1)} %get-tuple-element.9.high_ref, bf16[1024,1024]{1,0:T(8,128)(2,1)} %get-tuple-element.10.low_ref), custom_call_target="tpu_custom_call" | custom-call | tf_op jit(solution)/shard_map/pallas_call | solution.py:350
  80.0 19.4 %shard_map.125.in_ref = f32[32,32,512]{2,1,0:T(8,128)S(1)} custom-call(f32[32,32,512]{2,1,0:T(8,128)S(1)} %shard_map.123.in_ref, bf16[1024,1024]{1,0:T(8,128)(2,1)} %get-tuple-element.11.high_ref, bf16[1024,1024]{1,0:T(8,128)(2,1)} %get-tuple-element.12.low_ref, f32[1,1024]{1,0:T(1,128)S(1)} %bitcast.16, f32[32,1]{1,0:T(8,128)S(1)} %copy.14.values_y_ref, ...), custom_call_target="tpu_custom_call" | custom-call | tf_op jit(solution)/shard_map/pallas_call | solution.py:466
  99.4 65.0 %shard_map.126 = f32[4,512,256]{2,1,0:T(8,128)S(1)} custom-call(f32[32,32,512]{2,1,0:T(8,128)S(1)} %shard_map.125.in_ref, bf16[1024,1024]{1,0:T(8,128)(2,1)} %get-tuple-element.9.high_ref, bf16[1024,1024]{1,0:T(8,128)(2,1)} %get-tuple-element.10.low_ref), custom_call_target="tpu_custom_call" | custom-call | tf_op jit(solution)/shard_map/pallas_call | solution.py:350
  164.5 1.3 copy-done.2
  165.8 20.6 %shard_map.127 = (f32[16,128,256]{2,1,0:T(8,128)S(1)}, f32[16,128,256]{2,1,0:T(8,128)S(1)}, f32[4,16,32,256]{3,2,1,0:T(8,128)}) custom-call(f32[4,16,32,256]{3,2,1,0:T(8,128)} %bitcast.13, f32[16,128,256]{2,1,0:T(8,128)} %conduct_ref.3, s32[16,128,256]{2,1,0:T(8,128)} %active_ref.3, f32[16,128,256]{2,1,0:T(8,128)} %residual_ref.1, ...), custom_call_target="tpu_custom_call" | custom-call | tf_op jit(solution)/shard_map/pallas_call | solution.py:158
  186.4 1.3 copy-done.3
  187.7 1.3 copy-done.4
  189.1 1.6 copy-done.5
  190.7 59.9 %shard_map.128.in_ref = f32[32,32,512]{2,1,0:T(8,128)S(1)} custom-call(f32[4,512,256]{2,1,0:T(8,128)S(1)} %bitcast.15, bf16[1024,1024]{1,0:T(8,128)(2,1)} %get-tuple-element.9.high_ref, bf16[1024,1024]{1,0:T(8,128)(2,1)} %get-tuple-element.10.low_ref), custom_call_target="tpu_custom_call" | custom-call | tf_op jit(solution)/shard_map/pallas_call | solution.py:350
  250.6 19.6 %shard_map.129.in_ref = f32[32,32,512]{2,1,0:T(8,128)S(1)} custom-call(f32[32,32,512]{2,1,0:T(8,128)S(1)} %shard_map.128.in_ref, bf16[1024,1024]{1,0:T(8,128)(2,1)} %get-tuple-element.11.high_ref, bf16[1024,1024]{1,0:T(8,128)(2,1)} %get-tuple-element.12.low_ref, f32[1,1024]{1,0:T(1,128)S(1)} %bitcast.17, f32[32,1]{1,0:T(8,128)S(1)} %copy.14.values_y_ref, ...), custom_call_target="tpu_custom_call" | custom-call | tf_op jit(solution)/shard_map/pallas_call | solution.py:466
  270.1 63.1 %shard_map.130 = f32[4,512,256]{2,1,0:T(8,128)S(1)} custom-call(f32[32,32,512]{2,1,0:T(8,128)S(1)} %shard_map.129.in_ref, bf16[1024,1024]{1,0:T(8,128)(2,1)} %get-tuple-element.9.high_ref, bf16[1024,1024]{1,0:T(8,128)(2,1)} %get-tuple-element.10.low_ref), custom_call_target="tpu_custom_call" | custom-call | tf_op jit(solution)/shard_map/pallas_call | solution.py:350
  333.3 1.3 copy-done.1
  334.6 20.1 %shard_map.131 = (f32[16,128,256]{2,1,0:T(8,128)S(1)}, f32[16,128,256]{2,1,0:T(8,128)S(1)}) custom-call(f32[4,16,32,256]{3,2,1,0:T(8,128)} %bitcast.12, f32[16,128,256]{2,1,0:T(8,128)} %conduct_ref.3, s32[16,128,256]{2,1,0:T(8,128)} %active_ref.3, f32[16,128,256]{2,1,0:T(8,128)} %copy-done.4, f32[16,128,256]{2,1,0:T(8,128)} %copy-done.3), custom_call_target="tpu_custom_call" | custom-call | tf_op jit(solution)/shard_map/pallas_call | solution.py:158
  354.7 1.3 copy.19
  356.0 1.3 copy.20
  (13 shorter events, 0.0 us)
Async XLA Ops:
  0.6 0.7 copy-start
  17.7 62.3 %copy-start.6 = (f32[1024]{0:T(1024)S(1)}, f32[1024]{0:T(1024)}, u32[]{:S(2)}) copy-start(f32[1024]{0:T(1024)} %param.16) | copy-start | bytes 12292
  17.7 62.3 %copy-start.8 = (f32[16]{0:T(128)S(1)}, f32[16]{0:T(128)}, u32[]{:S(2)}) copy-start(f32[16]{0:T(128)} %diag_ref.3) | copy-start | bytes 196
  17.7 62.3 %copy-start.9 = (f32[15]{0:T(128)S(1)}, f32[15]{0:T(128)}, u32[]{:S(2)}) copy-start(f32[15]{0:T(128)} %coup_ref.3) | copy-start | bytes 184
  99.4 66.4 %copy-start.7 = (f32[256]{0:T(256)S(1)}, f32[256]{0:T(256)}, u32[]{:S(2)}) copy-start(f32[256]{0:T(256)} %param.18) | copy-start | bytes 3076
  164.4 1.3 copy-start.2
  186.4 1.3 copy-start.3
  187.7 1.3 copy-start.4
  189.1 1.6 copy-start.5
  333.3 1.3 copy-start.1

commit v4 on v3

--- a/solution.py
+++ b/solution.py
@@ -182,20 +182,13 @@
     return one(first[0], second[0]) + (one(first[0], second[1]) + one(first[1], second[0]))
 
 
-def split_kernel(in_ref, high_ref, low_ref):
-    high_ref[...], low_ref[...] = split(in_ref[...])
-
-
-def split_matrix(matrix):
-    rows, columns = matrix.shape
-    spec = pl.BlockSpec((rows // 8, columns), lambda i: (i, 0))
-    return pl.pallas_call(
-        split_kernel,
-        grid=(8,),
-        out_shape=[jax.ShapeDtypeStruct(matrix.shape, jnp.bfloat16)] * 2,
-        in_specs=[spec],
-        out_specs=[spec, spec],
-    )(matrix)
+def split_matrix(in_ref, high_ref, low_ref):
+    height = 64
+
+    @pl.loop(0, in_ref.shape[0] // height)
+    def _(step):
+        rows = pl.ds(pl.multiple_of(step * height, height), height)
+        high_ref[rows, :], low_ref[rows, :] = split(in_ref[rows, :])
 
 
 MESH = pl.DeviceIdType.MESH
@@ -260,8 +253,19 @@
     return copies
 
 
+def first_forward_kernel(
+    in_ref, y_ref, x_ref, out_ref, high_y_ref, low_y_ref, high_x_ref, low_x_ref, *scratch
+):
+    forward_kernel(
+        in_ref, high_y_ref, low_y_ref, out_ref, *scratch,
+        before=lambda: split_matrix(y_ref, high_y_ref, low_y_ref),
+        after=lambda: split_matrix(x_ref, high_x_ref, low_x_ref),
+    )
+
+
 def forward_kernel(
-    in_ref, high_ref, low_ref, out_ref, got, lines, high_in, low_in, send_x, recv_x, send_all, recv_all
+    in_ref, high_ref, low_ref, out_ref, got, lines, high_in, low_in, send_x, recv_x, send_all, recv_all,
+    before=None, after=None,
 ):
     sources, count, part = in_ref.shape
     devices, modes, _ = out_ref.shape
@@ -276,6 +280,8 @@
         for copy in copies[-1]:
             copy.start()
     got[ix] = in_ref[ix]
+    if before:
+        before()
     for chunk in range(chunks):
         rows = slice(chunk * LANES, (chunk + 1) * LANES)
         for copy in copies[chunk]:
@@ -297,6 +303,8 @@
 
         send_to_all(lines, out_ref, rows, send_all.at[chunk], recv_all.at[chunk])
         out_ref[me, :, rows] = lines[me, :, rows]
+    if after:
+        after()
     for chunk in range(chunks):
         rows = slice(chunk * LANES, (chunk + 1) * LANES)
         for copy in copies[chunk]:
@@ -347,11 +355,18 @@
     chunks = count // LANES
     rows_vmem, lines_vmem = VMEM(rows_shape, jnp.float32), VMEM(lines_shape, jnp.float32)
     row_sems = pltpu.SemaphoreType.DMA((chunks, rows_shape[0] - 1))
+    vmem = pl.BlockSpec(memory_space=VMEM)
+    out_shape = jax.ShapeDtypeStruct(lines_shape if forward else rows_shape, jnp.float32)
+    out_specs = vmem
+    if kernel is first_forward_kernel:
+        parts = [jax.ShapeDtypeStruct(matrix.shape, jnp.bfloat16) for matrix in (high, low)]
+        out_shape = [out_shape, parts[0], parts[0], parts[1], parts[1]]
+        out_specs = [vmem] * 5
     return pl.pallas_call(
         kernel,
-        out_shape=jax.ShapeDtypeStruct(lines_shape if forward else rows_shape, jnp.float32),
-        in_specs=[pl.BlockSpec(memory_space=VMEM)] * 3,
-        out_specs=pl.BlockSpec(memory_space=VMEM),
+        out_shape=out_shape,
+        in_specs=[vmem] * 3,
+        out_specs=out_specs,
         scratch_shapes=([rows_vmem, lines_vmem] if forward else [lines_vmem, rows_vmem])
         + [VMEM((LANES, size), jnp.bfloat16)] * 2
         + [row_sems] * 2
@@ -492,8 +507,6 @@
     levels, rows, part_y = right_side.shape
     part_x = rows // columns
     modes = vectors_y.shape[1] // devices
-    high_x, low_x = split_matrix(vectors_x)
-    high_y, low_y = split_matrix(vectors_y)
     start = (lax.axis_index("gy") * columns + lax.axis_index("gx")) * modes
     local_values = lax.dynamic_slice_in_dim(values_y, start, modes, 0)
     adjoint = None
@@ -503,9 +516,15 @@
     for iteration in range(ITERS):
         scaled = scaled.reshape(columns, levels * part_x, part_y)
         lines_shape = (devices, modes, levels * part_x)
-        got = y_transform(
-            forward_kernel, ITERS, scaled, high_y, low_y, scaled.shape, lines_shape, True
-        )
+        if iteration == 0:
+            got, high_y, low_y, high_x, low_x = y_transform(
+                first_forward_kernel, ITERS + 2, scaled, vectors_y, vectors_x, scaled.shape,
+                lines_shape, True,
+            )
+        else:
+            got = y_transform(
+                forward_kernel, ITERS, scaled, high_y, low_y, scaled.shape, lines_shape, True
+            )
         solved = middle(
             got, high_x, low_x, values_x, local_values, vertical_diag, vertical_coupling
         )

time: 358 us -> 351 us (0.980)
  Pallas kernels: 343 us -> 334 us
    pallas_call x6 -> x4, Pallas kernels: 264 us -> 255 us  [y_transform(): pl.pallas_call(kernel, out_shape=out_shape, in_specs=[vmem] * 3, out_spec...]
    unnamed x22 -> x24, local copies, waits for them, and re-layouts: 10.2 us -> 11.5 us
where the time goes in v4:
time: 351 us
  Pallas kernels  334 us (95%)
  local copies, waits for them, and re-layouts  13.9 us (4%)
    pallas_call x4, Pallas kernels, y_transform(): pl.pallas_call(kernel, out_shape=out_shape, in_specs=[vmem] * 3, out_spec...  255 us
    pallas_call x2, Pallas kernels, apply_update(): pl.pallas_call(functools.partial(apply_kernel, first, scale), out_shape=o...  40.6 us
    pallas_call x2, Pallas kernels, middle(): pl.pallas_call(middle_kernel, out_shape=jax.ShapeDtypeStruct(values.shape...  38.9 us
    unnamed x24, local copies, waits for them, and re-layouts  11.5 us

profile of v4, /device:TPU:0, one launch (start us, length us, event | category | flops | bytes accessed | tf_op | source)
XLA Modules:
  0.0 350.9 jit_solution(17794959619815661635)
XLA Ops:
  0.6 0.0 copy-start
  0.7 0.7 copy-done
  1.3 0.1 dynamic-slice_bitcast_fusion
  1.4 0.1 copy.14.values_y_ref
  1.5 0.8 copy.15.refs_0_
  2.2 1.9 multiply_multiply_fusion
  4.2 1.5 copy.13
  5.6 66.7 %shard_map.122 = (f32[32,32,512]{2,1,0:T(8,128)S(1)}, bf16[1024,1024]{1,0:T(8,128)(2,1)S(1)}, bf16[1024,1024]{1,0:T(8,128)(2,1)}, bf16[1024,1024]{1,0:T(8,128)(2,1)}, bf16[1024,1024]{1,0:T(8,128)(2,1)}) custom-call(f32[4,512,256]{2,1,0:T(8,128)} %bitcast.18, f32[1024,1024]{1,0:T(8,128)} %y_ref.1, f32[1024,1024]{1,0:T(8,128)} %x_ref.1), custom_call_target="tpu_custom_call" | custom-call | tf_op jit(solution)/shard_map/pallas_call | solution.py:365
  72.3 0.0 copy-start.1
  72.3 1.3 copy-done.1
  73.6 19.4 %shard_map.123.in_ref = f32[32,32,512]{2,1,0:T(8,128)S(1)} custom-call(f32[32,32,512]{2,1,0:T(8,128)S(1)} %get-tuple-element.10.in_ref, bf16[1024,1024]{1,0:T(8,128)(2,1)} %get-tuple-element.11.high_ref, bf16[1024,1024]{1,0:T(8,128)(2,1)} %get-tuple-element.12.low_ref, f32[1,1024]{1,0:T(1,128)S(1)} %bitcast.15, f32[32,1]{1,0:T(8,128)S(1)} %copy.14.values_y_ref, ...), custom_call_target="tpu_custom_call" | custom-call | tf_op jit(solution)/shard_map/pallas_call | solution.py:481
  93.0 65.0 %shard_map.124 = f32[4,512,256]{2,1,0:T(8,128)S(1)} custom-call(f32[32,32,512]{2,1,0:T(8,128)S(1)} %shard_map.123.in_ref, bf16[1024,1024]{1,0:T(8,128)(2,1)} %copy-done.1, bf16[1024,1024]{1,0:T(8,128)(2,1)} %get-tuple-element.14.low_ref), custom_call_target="tpu_custom_call" | custom-call | tf_op jit(solution)/shard_map/pallas_call | solution.py:365
  158.1 1.3 copy-done.3
  159.4 20.6 %shard_map.125 = (f32[16,128,256]{2,1,0:T(8,128)S(1)}, f32[16,128,256]{2,1,0:T(8,128)S(1)}, f32[4,16,32,256]{3,2,1,0:T(8,128)}) custom-call(f32[4,16,32,256]{3,2,1,0:T(8,128)} %bitcast.13, f32[16,128,256]{2,1,0:T(8,128)} %conduct_ref.3, s32[16,128,256]{2,1,0:T(8,128)} %active_ref.3, f32[16,128,256]{2,1,0:T(8,128)} %residual_ref.1, ...), custom_call_target="tpu_custom_call" | custom-call | tf_op jit(solution)/shard_map/pallas_call | solution.py:158
  180.0 1.3 copy-done.4
  181.3 1.3 copy-done.5
  182.7 1.6 copy-done.6
  184.3 59.9 %shard_map.126.in_ref = f32[32,32,512]{2,1,0:T(8,128)S(1)} custom-call(f32[4,512,256]{2,1,0:T(8,128)S(1)} %bitcast.14, bf16[1024,1024]{1,0:T(8,128)(2,1)} %copy-done.1, bf16[1024,1024]{1,0:T(8,128)(2,1)} %get-tuple-element.14.low_ref), custom_call_target="tpu_custom_call" | custom-call | tf_op jit(solution)/shard_map/pallas_call | solution.py:365
  244.2 19.6 %shard_map.127.in_ref = f32[32,32,512]{2,1,0:T(8,128)S(1)} custom-call(f32[32,32,512]{2,1,0:T(8,128)S(1)} %shard_map.126.in_ref, bf16[1024,1024]{1,0:T(8,128)(2,1)} %get-tuple-element.11.high_ref, bf16[1024,1024]{1,0:T(8,128)(2,1)} %get-tuple-element.12.low_ref, f32[1,1024]{1,0:T(1,128)S(1)} %bitcast.16, f32[32,1]{1,0:T(8,128)S(1)} %copy.14.values_y_ref, ...), custom_call_target="tpu_custom_call" | custom-call | tf_op jit(solution)/shard_map/pallas_call | solution.py:481
  263.7 63.2 %shard_map.128 = f32[4,512,256]{2,1,0:T(8,128)S(1)} custom-call(f32[32,32,512]{2,1,0:T(8,128)S(1)} %shard_map.127.in_ref, bf16[1024,1024]{1,0:T(8,128)(2,1)} %copy-done.1, bf16[1024,1024]{1,0:T(8,128)(2,1)} %get-tuple-element.14.low_ref), custom_call_target="tpu_custom_call" | custom-call | tf_op jit(solution)/shard_map/pallas_call | solution.py:365
  327.0 1.3 copy-done.2
  328.3 20.0 %shard_map.129 = (f32[16,128,256]{2,1,0:T(8,128)S(1)}, f32[16,128,256]{2,1,0:T(8,128)S(1)}) custom-call(f32[4,16,32,256]{3,2,1,0:T(8,128)} %bitcast.12, f32[16,128,256]{2,1,0:T(8,128)} %conduct_ref.3, s32[16,128,256]{2,1,0:T(8,128)} %active_ref.3, f32[16,128,256]{2,1,0:T(8,128)} %copy-done.5, f32[16,128,256]{2,1,0:T(8,128)} %copy-done.4), custom_call_target="tpu_custom_call" | custom-call | tf_op jit(solution)/shard_map/pallas_call | solution.py:158
  348.3 1.3 copy.19
  349.6 1.3 copy.20
  (13 shorter events, 0.0 us)
Async XLA Ops:
  0.6 0.7 copy-start
  5.6 68.0 %copy-start.7 = (f32[1024]{0:T(1024)S(1)}, f32[1024]{0:T(1024)}, u32[]{:S(2)}) copy-start(f32[1024]{0:T(1024)} %param.16) | copy-start | bytes 12292
  5.6 68.0 %copy-start.9 = (f32[16]{0:T(128)S(1)}, f32[16]{0:T(128)}, u32[]{:S(2)}) copy-start(f32[16]{0:T(128)} %diag_ref.3) | copy-start | bytes 196
  5.6 68.0 %copy-start.10 = (f32[15]{0:T(128)S(1)}, f32[15]{0:T(128)}, u32[]{:S(2)}) copy-start(f32[15]{0:T(128)} %coup_ref.3) | copy-start | bytes 184
  72.3 1.3 copy-start.1
  93.0 66.4 %copy-start.8 = (f32[256]{0:T(256)S(1)}, f32[256]{0:T(256)}, u32[]{:S(2)}) copy-start(f32[256]{0:T(256)} %param.18) | copy-start | bytes 3076
  158.1 1.3 copy-start.3
  180.0 1.3 copy-start.4
  181.3 1.3 copy-start.5
  182.7 1.6 copy-start.6
  326.9 1.3 copy-start.2
